TPU v7x, 512 devices: a whole 4x4x16 slice. The times are simulated.
512 devices in a mesh: ens: 16 (over z), grid: 32 (over x, y, core).
Axes of the slice: x: 4, y: 4, z: 16, core: 2. Of those that a mesh axis runs over, the one named last changes fastest.
Arguments:
- hidden_mesh_vectors: bfloat16 [16, 1024, 1024], P('ens', 'grid'), may hold values from -6 to 6
- grid_embed: bfloat16 [16384, 1024], P('grid'), may hold values from -6 to 6
- w_src: bfloat16 [1024, 1024], replicated, may hold values from -0.1875 to 0.1875
- readout_matrix: bfloat16 [99, 1024], replicated, may hold values from -0.1875 to 0.1875
- b_out: float32 [99], replicated, may hold values from -3 to 3
- verifying_reanalysis: float32 [99, 16384], P(None, 'grid'), may hold values from -6 to 6
- var_w: float32 [99], replicated, may hold values from 0.1 to 1
- area_w: float32 [16384], P('grid'), may hold values from 0.25 to 7.5
- edge_src: int32 [49152], P('grid'), may hold values from 0 to 1023, as said below
- edge_dst: int32 [49152], P('grid'), may hold values from 0 to 512, as said below
Outputs:
- mesh_vector_derivative: float32 [16, 1024, 1024], P('ens', 'grid')
- loss: float32 [], replicated
Inputs may be any that keep to these rules, and one draw needn't show every extreme that they name: `edge_src`: each slot of shard s that is not empty has a source between (s - 1) * 32 and (s + 2) * 32 - 1; an empty slot has source s * 32. `edge_dst`: the value 512 marks an empty slot; in each shard the non-empty slots come first, at least half of the 1536 slots are non-empty, and some shard has none empty.
All inputs are finite; a program needn't handle non-finite values.
Results may differ from a plain program's by a relative error of at most 0.0074.
Values may be sent and summed in bfloat16 or wider, within the bound.
No kernel may reach another device: no remote copies, remote signals or barrier semaphores. Data moves between devices by JAX's collectives and lax.ppermute only.
A program may use at most 64 MiB of HBM per device.

v0:
```python
import jax
import jax.numpy as jnp
from jax import lax
from jax.sharding import PartitionSpec as P

smooth_width = 0.1
batch_axes_prefix = (((0,), (0,)), ((), ()))


def padded(cells, sides, width):
    for axis, dim in sides:
        count = lax.axis_size(axis)
        ends = count - 1
        head = lax.slice_in_dim(cells, 0, width, axis=dim)
        tail = lax.slice_in_dim(cells, cells.shape[dim] - width, cells.shape[dim], axis=dim)
        cells = jnp.concatenate(
            [
                lax.ppermute(tail, axis, [(i, (i + 1) % count) for i in range(ends)]),
                cells,
                lax.ppermute(head, axis, [((i + 1) % count, i) for i in range(ends)]),
            ],
            axis=dim,
        )
    return cells


def shifted(block, axis, distance):
    devices = range(lax.axis_size(axis))
    route = [((i - distance) % len(devices), i) for i in devices]
    return lax.ppermute(block, axis, route)


def from_behind(block, axis, distance):
    devices = range(lax.axis_size(axis))
    route = [(i - distance, i) for i in devices if i - distance in devices]
    return lax.ppermute(block, axis, route)


def softened_magnitude(dispersion_contribution):
    return (
        jnp.sqrt(dispersion_contribution * dispersion_contribution + smooth_width * smooth_width)
        - smooth_width
    )


def softened_derivative(dispersion_contribution):
    return dispersion_contribution / jnp.sqrt(
        dispersion_contribution * dispersion_contribution + smooth_width * smooth_width
    )


def shards(
    hidden_mesh_vectors,
    grid_embed,
    w_src,
    readout_matrix,
    b_out,
    verifying_reanalysis,
    var_w,
    area_w,
    edge_src,
    edge_dst,
):
    nodes_dev = hidden_mesh_vectors.shape[1]
    points_dev = grid_embed.shape[0]
    variables = readout_matrix.shape[0]
    realization_maps = lax.axis_size("ens")
    grid_rank = lax.axis_index("grid")
    window_start = (grid_rank - 1) * nodes_dev
    local_src = edge_src - window_start
    src_table = (jnp.arange(3 * nodes_dev, dtype=jnp.int32)[:, None] == local_src[None, :]).astype(
        jnp.bfloat16
    )
    dst_table = (jnp.arange(points_dev, dtype=jnp.int32)[:, None] == edge_dst[None, :]).astype(
        jnp.bfloat16
    )
    window_nodes = padded(hidden_mesh_vectors[0], (("grid", 0),), nodes_dev)
    window_proj = jnp.dot(window_nodes, w_src, preferred_element_type=jnp.float32).astype(
        jnp.bfloat16
    )
    preact = lax.dot_general(
        src_table, window_proj, batch_axes_prefix, preferred_element_type=jnp.float32
    )
    preact = preact + lax.dot_general(
        dst_table, grid_embed, batch_axes_prefix, preferred_element_type=jnp.float32
    )
    message = (preact * jax.nn.sigmoid(preact)).astype(jnp.bfloat16)
    aggregate = jnp.dot(dst_table, message, preferred_element_type=jnp.float32).astype(jnp.bfloat16)
    prediction_snapshot = (
        lax.dot_general(
            readout_matrix, aggregate, (((1,), (1,)), ((), ())), preferred_element_type=jnp.float32
        )
        + b_out[:, None]
    )
    scaling_coefficient = var_w[:, None] * area_w[None, :]
    prediction_misfit = prediction_snapshot - verifying_reanalysis
    empty_variable_canvas = jnp.zeros_like(prediction_snapshot)
    half_turns = realization_maps // 2
    couple_fraction = empty_variable_canvas
    couple_derivative = empty_variable_canvas
    for realization_offset in range(1, half_turns + 1):
        other_realization = shifted(prediction_snapshot, "ens", realization_offset)
        dispersion_contribution = prediction_snapshot - other_realization
        slope_now = softened_derivative(dispersion_contribution)
        if realization_offset < half_turns:
            couple_fraction = couple_fraction + softened_magnitude(dispersion_contribution)
            returned = shifted(-slope_now, "ens", -realization_offset)
            couple_derivative = couple_derivative + slope_now + returned
        else:
            couple_fraction = couple_fraction + 0.5 * softened_magnitude(dispersion_contribution)
            couple_derivative = couple_derivative + slope_now
    local_loss = jnp.sum(
        scaling_coefficient
        * (softened_magnitude(prediction_misfit) - couple_fraction / (realization_maps - 1))
    )
    summed_loss = lax.psum(local_loss, ("ens", "grid"))
    loss = summed_loss / (realization_maps * variables * points_dev * lax.axis_size("grid"))
    prediction_derivative = (
        scaling_coefficient
        * (softened_derivative(prediction_misfit) - couple_derivative / (realization_maps - 1))
    ).astype(jnp.bfloat16)
    grad_agg = lax.dot_general(
        prediction_derivative, readout_matrix, batch_axes_prefix, preferred_element_type=jnp.float32
    ).astype(jnp.bfloat16)
    grad_msg = lax.dot_general(
        dst_table, grad_agg, batch_axes_prefix, preferred_element_type=jnp.float32
    )
    sigmoid_pre = jax.nn.sigmoid(preact)
    grad_pre = (grad_msg * sigmoid_pre * (1.0 + preact * (1.0 - sigmoid_pre))).astype(jnp.bfloat16)
    grad_window = jnp.dot(src_table, grad_pre, preferred_element_type=jnp.float32)
    below_rows = grad_window[:nodes_dev]
    own_rows = grad_window[nodes_dev : 2 * nodes_dev]
    above_rows = grad_window[2 * nodes_dev :]
    from_above = from_behind(below_rows, "grid", -1)
    from_below = from_behind(above_rows, "grid", 1)
    grad_proj = (own_rows + from_above + from_below).astype(jnp.bfloat16)
    grad_nodes = lax.dot_general(
        grad_proj, w_src, (((1,), (1,)), ((), ())), preferred_element_type=jnp.float32
    )
    return (grad_nodes[None], loss)


def solution(mesh):
    in_specs = (
        P("ens", "grid", None),
        P("grid", None),
        P(),
        P(),
        P(),
        P(None, "grid"),
        P(),
        P("grid"),
        P("grid"),
        P("grid"),
    )
    out_specs = (P("ens", "grid", None), P())
    return jax.shard_map(shards, mesh=mesh, in_specs=in_specs, out_specs=out_specs, check_vma=False)
```

profile of v0, /device:TPU:6, one launch (start us, length us, event | category | flops | bytes accessed | tf_op | source)
XLA Modules:
  0.0 443.7 jit_solution(9767240126155769026)
XLA Ops:
  0.6 0.0 copy-start
  0.6 0.0 copy-start.2
  0.7 0.0 copy-start.3
  0.7 4.8 %collective-permute-start.1 = (bf16[32,1024]{1,0:T(8,128)(2,1)}, bf16[32,1024]{1,0:T(8,128)(2,1)S(1)}, u32[]{:S(2)}, u32[]{:S(2)}) collective-permute-start(bf16[32,1024]{1,0:T(8,128)(2,1)} %bitcast.11), channel_id=1, source_target_pairs={{1,0},{2,1},{3,2},{4,3},{5,4},{6,5},{7,6},{8,7},{9,8},{10,9},{11,1... | collective-permute-start | bytes 196616 | tf_op jit(solution)/shard_map/ppermute | solution.py:20
  5.4 1.9 collective-permute-start
  7.4 5.8 %fusion.1 = f32[1536,1024]{1,0:T(8,128)} fusion(bf16[512,1024]{1,0:T(8,128)(2,1)} %param.11, s32[1536]{0:T(1024)} %param.19), kind=kOutput, calls=%fused_computation.6 | convolution fusion | flops 1611399168 | bytes 7346176 | tf_op jit(solution)/shard_map/dot_general | solution.py:84
  13.1 0.0 copy-done.3
  13.1 0.0 copy-start.6
  13.1 0.0 copy-start.7
  13.1 0.0 copy-start.8
  13.1 0.0 collective-permute-done.1
  13.2 0.2 collective-permute-done
  13.3 0.0 copy-done
  13.3 0.0 copy-done.2
  13.3 6.7 %convolution_add_fusion = f32[1536,1024]{1,0:T(8,128)} fusion(f32[1536,1024]{1,0:T(8,128)} %fusion.1, bf16[1024,1024]{1,0:T(8,128)(2,1)S(1)} %copy-done, s32[1536]{0:T(1024)S(1)} %broadcast_subtract_fusion, bf16[32,1024]{1,0:T(8,128)(2,1)S(1)} %collective-permute-done.1, bf16[32,1024]{1,0:T(8,128)(2,1)S(1)} %bitcast.13, ...), kind=kOutput, calls=%fused_computation.3 | convolution fusion | flops 505724928 | bytes 14882816 | tf_op jit(solution)/shard_map/dot_general | solution.py:81
  20.1 0.0 copy-done.6
  20.1 0.0 copy-done.7
  20.1 0.0 copy-done.8
  20.1 0.0 copy-start.1
  20.1 0.0 copy-start.4
  20.1 0.0 copy-start.5
  20.1 5.3 %fusion.9 = f32[99,512]{1,0:T(8,128)S(1)} fusion(bf16[99,1024]{1,0:T(8,128)(2,1)S(1)} %copy-done.6, f32[1536,1024]{1,0:T(8,128)} %convolution_add_fusion, s32[1536]{0:T(1024)S(1)} %copy-done.7, f32[99]{0:T(128)S(1)} %copy-done.8), kind=kOutput, calls=%fused_computation.16 | convolution fusion | flops 1723647488 | bytes 6703500 | tf_op jit(solution)/shard_map/dot_general | solution.py:90
  25.5 10.5 %collective-permute-start.10 = (f32[99,512]{1,0:T(8,128)S(1)}, f32[99,512]{1,0:T(8,128)S(1)}, u32[]{:S(2)}, u32[]{:S(2)}) collective-permute-start(f32[99,512]{1,0:T(8,128)S(1)} %fusion.9), channel_id=1, source_target_pairs={{352,0},{384,32},{416,64},{448,96},{480,128},{0,160},{32,192},{64,... | collective-permute-start | bytes 608264 | tf_op jit(solution)/shard_map/ppermute | solution.py:30
  35.9 9.6 %collective-permute-start.14 = (f32[99,512]{1,0:T(8,128)S(1)}, f32[99,512]{1,0:T(8,128)S(1)}, u32[]{:S(2)}, u32[]{:S(2)}) collective-permute-start(f32[99,512]{1,0:T(8,128)S(1)} %fusion.9), channel_id=1, source_target_pairs={{288,0},{320,32},{352,64},{384,96},{416,128},{448,160},{480,192},{... | collective-permute-start | bytes 608264 | tf_op jit(solution)/shard_map/ppermute | solution.py:30
  45.5 1.9 collective-permute-start.8
  47.4 10.8 %collective-permute-start.16 = (f32[99,512]{1,0:T(8,128)S(1)}, f32[99,512]{1,0:T(8,128)S(1)}, u32[]{:S(2)}, u32[]{:S(2)}) collective-permute-start(f32[99,512]{1,0:T(8,128)S(1)} %fusion.9), channel_id=1, source_target_pairs={{256,0},{288,32},{320,64},{352,96},{384,128},{416,160},{448,192},{... | collective-permute-start | bytes 608264 | tf_op jit(solution)/shard_map/ppermute | solution.py:30
  58.2 3.8 collective-permute-start.6
  62.1 0.0 collective-permute-done.10
  62.1 13.1 %collective-permute-start.12 = (f32[99,512]{1,0:T(8,128)S(1)}, f32[99,512]{1,0:T(8,128)S(1)}, u32[]{:S(2)}, u32[]{:S(2)}) collective-permute-start(f32[99,512]{1,0:T(8,128)S(1)} %fusion.9), channel_id=1, source_target_pairs={{320,0},{352,32},{384,64},{416,96},{448,128},{480,160},{0,192},{32... | collective-permute-start | bytes 608264 | tf_op jit(solution)/shard_map/ppermute | solution.py:30
  75.2 30.3 %collective-permute-done.14 = f32[99,512]{1,0:T(8,128)S(1)} collective-permute-done((f32[99,512]{1,0:T(8,128)S(1)}, f32[99,512]{1,0:T(8,128)S(1)}, u32[]{:S(2)}, u32[]{:S(2)}) %collective-permute-start.14) | collective-permute-done | bytes 202784 | tf_op jit(solution)/shard_map/ppermute | solution.py:30
  105.5 1.9 collective-permute-start.4
  107.4 5.1 %collective-permute-done.8 = f32[99,512]{1,0:T(8,128)S(1)} collective-permute-done((f32[99,512]{1,0:T(8,128)S(1)}, f32[99,512]{1,0:T(8,128)S(1)}, u32[]{:S(2)}, u32[]{:S(2)}) %collective-permute-start.8) | collective-permute-done | bytes 202784 | tf_op jit(solution)/shard_map/ppermute | solution.py:30
  112.5 25.6 %collective-permute-start.2 = (f32[99,512]{1,0:T(8,128)S(1)}, f32[99,512]{1,0:T(8,128)S(1)}, u32[]{:S(2)}, u32[]{:S(2)}) collective-permute-start(f32[99,512]{1,0:T(8,128)S(1)} %fusion.9), channel_id=1, source_target_pairs={{480,0},{0,32},{32,64},{64,96},{96,128},{128,160},{160,192},{192,2... | collective-permute-start | bytes 608264 | tf_op jit(solution)/shard_map/ppermute | solution.py:30
  138.1 3.7 collective-permute-done.16
  141.8 0.0 collective-permute-done.6
  141.8 25.1 %collective-permute-done.12 = f32[99,512]{1,0:T(8,128)S(1)} collective-permute-done((f32[99,512]{1,0:T(8,128)S(1)}, f32[99,512]{1,0:T(8,128)S(1)}, u32[]{:S(2)}, u32[]{:S(2)}) %collective-permute-start.12) | collective-permute-done | bytes 202784 | tf_op jit(solution)/shard_map/ppermute | solution.py:30
  166.9 11.9 %collective-permute-done.4 = f32[99,512]{1,0:T(8,128)S(1)} collective-permute-done((f32[99,512]{1,0:T(8,128)S(1)}, f32[99,512]{1,0:T(8,128)S(1)}, u32[]{:S(2)}, u32[]{:S(2)}) %collective-permute-start.4) | collective-permute-done | bytes 202784 | tf_op jit(solution)/shard_map/ppermute | solution.py:30
  178.8 4.0 collective-permute-done.2
  182.8 0.0 copy-done.1
  182.8 0.0 copy-done.4
  182.8 0.0 copy-done.5
  182.8 1.8 fusion.13
  184.6 9.3 %collective-permute-start.15 = (f32[99,512]{1,0:T(8,128)S(1)}, f32[99,512]{1,0:T(8,128)S(1)}, u32[]{:S(2)}, u32[]{:S(2)}) collective-permute-start(f32[99,512]{1,0:T(8,128)S(1)} %get-tuple-element.3), channel_id=1, source_target_pairs={{224,0},{256,32},{288,64},{320,96},{352,128},{384,160},{416,192},{... | collective-permute-start | bytes 608264 | tf_op jit(solution)/shard_map/ppermute | solution.py:30
  193.8 4.5 %collective-permute-start.13 = (f32[99,512]{1,0:T(8,128)S(1)}, f32[99,512]{1,0:T(8,128)S(1)}, u32[]{:S(2)}, u32[]{:S(2)}) collective-permute-start(f32[99,512]{1,0:T(8,128)S(1)} %get-tuple-element.4), channel_id=1, source_target_pairs={{192,0},{224,32},{256,64},{288,96},{320,128},{352,160},{384,192},{... | collective-permute-start | bytes 608264 | tf_op jit(solution)/shard_map/ppermute | solution.py:30
  198.3 4.2 collective-permute-start.11
  202.6 7.9 %collective-permute-start.9 = (f32[99,512]{1,0:T(8,128)S(1)}, f32[99,512]{1,0:T(8,128)S(1)}, u32[]{:S(2)}, u32[]{:S(2)}) collective-permute-start(f32[99,512]{1,0:T(8,128)S(1)} %get-tuple-element.6), channel_id=1, source_target_pairs={{128,0},{160,32},{192,64},{224,96},{256,128},{288,160},{320,192},{... | collective-permute-start | bytes 608264 | tf_op jit(solution)/shard_map/ppermute | solution.py:30
  210.5 5.1 %collective-permute-start.7 = (f32[99,512]{1,0:T(8,128)S(1)}, f32[99,512]{1,0:T(8,128)S(1)}, u32[]{:S(2)}, u32[]{:S(2)}) collective-permute-start(f32[99,512]{1,0:T(8,128)S(1)} %get-tuple-element.7), channel_id=1, source_target_pairs={{96,0},{128,32},{160,64},{192,96},{224,128},{256,160},{288,192},{3... | collective-permute-start | bytes 608264 | tf_op jit(solution)/shard_map/ppermute | solution.py:30
  215.5 22.8 %collective-permute-done.15 = f32[99,512]{1,0:T(8,128)S(1)} collective-permute-done((f32[99,512]{1,0:T(8,128)S(1)}, f32[99,512]{1,0:T(8,128)S(1)}, u32[]{:S(2)}, u32[]{:S(2)}) %collective-permute-start.15) | collective-permute-done | bytes 202784 | tf_op jit(solution)/shard_map/ppermute | solution.py:30
  238.3 1.9 collective-permute-start.5
  240.2 20.7 %collective-permute-done.13 = f32[99,512]{1,0:T(8,128)S(1)} collective-permute-done((f32[99,512]{1,0:T(8,128)S(1)}, f32[99,512]{1,0:T(8,128)S(1)}, u32[]{:S(2)}, u32[]{:S(2)}) %collective-permute-start.13) | collective-permute-done | bytes 202784 | tf_op jit(solution)/shard_map/ppermute | solution.py:30
  260.9 2.1 collective-permute-start.3
  263.0 20.5 %collective-permute-done.11 = f32[99,512]{1,0:T(8,128)S(1)} collective-permute-done((f32[99,512]{1,0:T(8,128)S(1)}, f32[99,512]{1,0:T(8,128)S(1)}, u32[]{:S(2)}, u32[]{:S(2)}) %collective-permute-start.11) | collective-permute-done | bytes 202784 | tf_op jit(solution)/shard_map/ppermute | solution.py:30
  283.5 11.9 %collective-permute-done.9 = f32[99,512]{1,0:T(8,128)S(1)} collective-permute-done((f32[99,512]{1,0:T(8,128)S(1)}, f32[99,512]{1,0:T(8,128)S(1)}, u32[]{:S(2)}, u32[]{:S(2)}) %collective-permute-start.9) | collective-permute-done | bytes 202784 | tf_op jit(solution)/shard_map/ppermute | solution.py:30
  295.4 13.0 %collective-permute-done.7 = f32[99,512]{1,0:T(8,128)S(1)} collective-permute-done((f32[99,512]{1,0:T(8,128)S(1)}, f32[99,512]{1,0:T(8,128)S(1)}, u32[]{:S(2)}, u32[]{:S(2)}) %collective-permute-start.7) | collective-permute-done | bytes 202784 | tf_op jit(solution)/shard_map/ppermute | solution.py:30
  308.4 7.8 %collective-permute-done.5 = f32[99,512]{1,0:T(8,128)S(1)} collective-permute-done((f32[99,512]{1,0:T(8,128)S(1)}, f32[99,512]{1,0:T(8,128)S(1)}, u32[]{:S(2)}, u32[]{:S(2)}) %collective-permute-start.5) | collective-permute-done | bytes 202784 | tf_op jit(solution)/shard_map/ppermute | solution.py:30
  316.2 4.5 %collective-permute-done.3 = f32[99,512]{1,0:T(8,128)S(1)} collective-permute-done((f32[99,512]{1,0:T(8,128)S(1)}, f32[99,512]{1,0:T(8,128)S(1)}, u32[]{:S(2)}, u32[]{:S(2)}) %collective-permute-start.3) | collective-permute-done | bytes 202784 | tf_op jit(solution)/shard_map/ppermute | solution.py:30
  320.6 2.3 convolution_convert_fusion
  322.9 6.8 %fusion.5 = f32[96,1024]{1,0:T(8,128)S(1)} fusion(f32[1536,1024]{1,0:T(8,128)} %convolution_add_fusion, bf16[512,1024]{1,0:T(8,128)(2,1)} %convolution_convert_fusion, s32[1536]{0:T(1024)S(1)} %copy-done.7, s32[1536]{0:T(1024)S(1)} %broadcast_subtract_fusion), kind=kOutput, calls=%fused_computation.10 | convolution fusion | flops 1927692288 | bytes 7745536 | tf_op jit(solution)/shard_map/dot_general | solution.py:130
  329.8 5.4 %collective-permute-start.17 = (f32[32,1024]{1,0:T(8,128)S(1)}, f32[32,1024]{1,0:T(8,128)S(1)}, u32[]{:S(2)}, u32[]{:S(2)}) collective-permute-start(f32[32,1024]{1,0:T(8,128)S(1)} %get-tuple-element.10), channel_id=1, source_target_pairs={{1,0},{2,1},{3,2},{4,3},{5,4},{6,5},{7,6},{8,7},{9,8},{10,9},{11,1... | collective-permute-start | bytes 393224 | tf_op jit(solution)/shard_map/ppermute | solution.py:36
  335.2 1.9 collective-permute-start.18
  337.2 103.3 %psum.7 = f32[]{:T(128)} all-reduce(f32[]{:T(128)} %get-tuple-element.2), channel_id=1, replica_groups=mesh['ens'=16,'grid'=32] {'ens','grid'}, use_global_device_ids=true, to_apply=%region_1.0 | all-reduce | flops 1 | bytes 8 | tf_op jit(solution)/shard_map/psum | solution.py:116
  441.1 0.0 collective-permute-done.17
  441.1 0.0 collective-permute-done.18
  441.1 1.4 convolution_bitcast_fusion
  (2 shorter events, 0.0 us)
Async XLA Ops:
  0.6 12.7 %copy-start = (bf16[1024,1024]{1,0:T(8,128)(2,1)S(1)}, bf16[1024,1024]{1,0:T(8,128)(2,1)}, u32[]{:S(2)}) copy-start(bf16[1024,1024]{1,0:T(8,128)(2,1)} %param.12) | copy-start | bytes 6291460
  0.6 12.7 %copy-start.2 = (bf16[1,32,1024]{2,1,0:T(8,128)(2,1)S(1)}, bf16[1,32,1024]{2,1,0:T(8,128)(2,1)}, u32[]{:S(2)}) copy-start(bf16[1,32,1024]{2,1,0:T(8,128)(2,1)} %param.10) | copy-start | bytes 196612
  0.7 12.5 %copy-start.3 = (s32[1536]{0:T(1024)S(1)}, s32[1536]{0:T(1024)}, u32[]{:S(2)}) copy-start(s32[1536]{0:T(1024)} %param.18) | copy-start | bytes 18436
  0.7 12.5 %collective-permute-start.1 = (bf16[32,1024]{1,0:T(8,128)(2,1)}, bf16[32,1024]{1,0:T(8,128)(2,1)S(1)}, u32[]{:S(2)}, u32[]{:S(2)}) collective-permute-start(bf16[32,1024]{1,0:T(8,128)(2,1)} %bitcast.11), channel_id=1, source_target_pairs={{1,0},{2,1},{3,2},{4,3},{5,4},{6,5},{7,6},{8,7},{9,8},{10,9},{11,1... | collective-permute-start | bytes 196616 | tf_op jit(solution)/shard_map/ppermute | solution.py:20
  5.4 7.9 %collective-permute-start = (bf16[32,1024]{1,0:T(8,128)(2,1)}, bf16[32,1024]{1,0:T(8,128)(2,1)S(1)}, u32[]{:S(2)}, u32[]{:S(2)}) collective-permute-start(bf16[32,1024]{1,0:T(8,128)(2,1)} %bitcast.12), channel_id=1, source_target_pairs={{0,1},{1,2},{2,3},{3,4},{4,5},{5,6},{6,7},{7,8},{8,9},{9,10},{10,1... | collective-permute-start | bytes 196616 | tf_op jit(solution)/shard_map/ppermute | solution.py:18
  13.1 7.0 %copy-start.6 = (bf16[99,1024]{1,0:T(8,128)(2,1)S(1)}, bf16[99,1024]{1,0:T(8,128)(2,1)}, u32[]{:S(2)}) copy-start(bf16[99,1024]{1,0:T(8,128)(2,1)} %param.13) | copy-start | bytes 608260
  13.1 7.0 %copy-start.7 = (s32[1536]{0:T(1024)S(1)}, s32[1536]{0:T(1024)}, u32[]{:S(2)}) copy-start(s32[1536]{0:T(1024)} %param.19) | copy-start | bytes 18436
  13.1 7.0 %copy-start.8 = (f32[99]{0:T(128)S(1)}, f32[99]{0:T(128)}, u32[]{:S(2)}) copy-start(f32[99]{0:T(128)} %param.14) | copy-start | bytes 1192
  20.1 162.7 %copy-start.1 = (f32[99,512]{1,0:T(8,128)S(1)}, f32[99,512]{1,0:T(8,128)}, u32[]{:S(2)}) copy-start(f32[99,512]{1,0:T(8,128)} %param.15) | copy-start | bytes 608260
  20.1 162.7 %copy-start.4 = (f32[512]{0:T(512)S(1)}, f32[512]{0:T(512)}, u32[]{:S(2)}) copy-start(f32[512]{0:T(512)} %param.17) | copy-start | bytes 6148
  20.1 162.7 %copy-start.5 = (f32[99]{0:T(128)S(1)}, f32[99]{0:T(128)}, u32[]{:S(2)}) copy-start(f32[99]{0:T(128)} %param.16) | copy-start | bytes 1192
  25.5 36.6 %collective-permute-start.10 = (f32[99,512]{1,0:T(8,128)S(1)}, f32[99,512]{1,0:T(8,128)S(1)}, u32[]{:S(2)}, u32[]{:S(2)}) collective-permute-start(f32[99,512]{1,0:T(8,128)S(1)} %fusion.9), channel_id=1, source_target_pairs={{352,0},{384,32},{416,64},{448,96},{480,128},{0,160},{32,192},{64,... | collective-permute-start | bytes 608264 | tf_op jit(solution)/shard_map/ppermute | solution.py:30
  35.9 69.5 %collective-permute-start.14 = (f32[99,512]{1,0:T(8,128)S(1)}, f32[99,512]{1,0:T(8,128)S(1)}, u32[]{:S(2)}, u32[]{:S(2)}) collective-permute-start(f32[99,512]{1,0:T(8,128)S(1)} %fusion.9), channel_id=1, source_target_pairs={{288,0},{320,32},{352,64},{384,96},{416,128},{448,160},{480,192},{... | collective-permute-start | bytes 608264 | tf_op jit(solution)/shard_map/ppermute | solution.py:30
  45.5 67.0 %collective-permute-start.8 = (f32[99,512]{1,0:T(8,128)S(1)}, f32[99,512]{1,0:T(8,128)S(1)}, u32[]{:S(2)}, u32[]{:S(2)}) collective-permute-start(f32[99,512]{1,0:T(8,128)S(1)} %fusion.9), channel_id=1, source_target_pairs={{384,0},{416,32},{448,64},{480,96},{0,128},{32,160},{64,192},{96,2... | collective-permute-start | bytes 608264 | tf_op jit(solution)/shard_map/ppermute | solution.py:30
  47.4 94.4 %collective-permute-start.16 = (f32[99,512]{1,0:T(8,128)S(1)}, f32[99,512]{1,0:T(8,128)S(1)}, u32[]{:S(2)}, u32[]{:S(2)}) collective-permute-start(f32[99,512]{1,0:T(8,128)S(1)} %fusion.9), channel_id=1, source_target_pairs={{256,0},{288,32},{320,64},{352,96},{384,128},{416,160},{448,192},{... | collective-permute-start | bytes 608264 | tf_op jit(solution)/shard_map/ppermute | solution.py:30
  58.2 83.6 %collective-permute-start.6 = (f32[99,512]{1,0:T(8,128)S(1)}, f32[99,512]{1,0:T(8,128)S(1)}, u32[]{:S(2)}, u32[]{:S(2)}) collective-permute-start(f32[99,512]{1,0:T(8,128)S(1)} %fusion.9), channel_id=1, source_target_pairs={{416,0},{448,32},{480,64},{0,96},{32,128},{64,160},{96,192},{128,2... | collective-permute-start | bytes 608264 | tf_op jit(solution)/shard_map/ppermute | solution.py:30
  62.1 104.8 %collective-permute-start.12 = (f32[99,512]{1,0:T(8,128)S(1)}, f32[99,512]{1,0:T(8,128)S(1)}, u32[]{:S(2)}, u32[]{:S(2)}) collective-permute-start(f32[99,512]{1,0:T(8,128)S(1)} %fusion.9), channel_id=1, source_target_pairs={{320,0},{352,32},{384,64},{416,96},{448,128},{480,160},{0,192},{32... | collective-permute-start | bytes 608264 | tf_op jit(solution)/shard_map/ppermute | solution.py:30
  105.5 73.4 %collective-permute-start.4 = (f32[99,512]{1,0:T(8,128)S(1)}, f32[99,512]{1,0:T(8,128)S(1)}, u32[]{:S(2)}, u32[]{:S(2)}) collective-permute-start(f32[99,512]{1,0:T(8,128)S(1)} %fusion.9), channel_id=1, source_target_pairs={{448,0},{480,32},{0,64},{32,96},{64,128},{96,160},{128,192},{160,2... | collective-permute-start | bytes 608264 | tf_op jit(solution)/shard_map/ppermute | solution.py:30
  112.5 70.4 %collective-permute-start.2 = (f32[99,512]{1,0:T(8,128)S(1)}, f32[99,512]{1,0:T(8,128)S(1)}, u32[]{:S(2)}, u32[]{:S(2)}) collective-permute-start(f32[99,512]{1,0:T(8,128)S(1)} %fusion.9), channel_id=1, source_target_pairs={{480,0},{0,32},{32,64},{64,96},{96,128},{128,160},{160,192},{192,2... | collective-permute-start | bytes 608264 | tf_op jit(solution)/shard_map/ppermute | solution.py:30
  184.6 53.7 %collective-permute-start.15 = (f32[99,512]{1,0:T(8,128)S(1)}, f32[99,512]{1,0:T(8,128)S(1)}, u32[]{:S(2)}, u32[]{:S(2)}) collective-permute-start(f32[99,512]{1,0:T(8,128)S(1)} %get-tuple-element.3), channel_id=1, source_target_pairs={{224,0},{256,32},{288,64},{320,96},{352,128},{384,160},{416,192},{... | collective-permute-start | bytes 608264 | tf_op jit(solution)/shard_map/ppermute | solution.py:30
  193.8 67.1 %collective-permute-start.13 = (f32[99,512]{1,0:T(8,128)S(1)}, f32[99,512]{1,0:T(8,128)S(1)}, u32[]{:S(2)}, u32[]{:S(2)}) collective-permute-start(f32[99,512]{1,0:T(8,128)S(1)} %get-tuple-element.4), channel_id=1, source_target_pairs={{192,0},{224,32},{256,64},{288,96},{320,128},{352,160},{384,192},{... | collective-permute-start | bytes 608264 | tf_op jit(solution)/shard_map/ppermute | solution.py:30
  198.3 85.2 %collective-permute-start.11 = (f32[99,512]{1,0:T(8,128)S(1)}, f32[99,512]{1,0:T(8,128)S(1)}, u32[]{:S(2)}, u32[]{:S(2)}) collective-permute-start(f32[99,512]{1,0:T(8,128)S(1)} %get-tuple-element.5), channel_id=1, source_target_pairs={{160,0},{192,32},{224,64},{256,96},{288,128},{320,160},{352,192},{... | collective-permute-start | bytes 608264 | tf_op jit(solution)/shard_map/ppermute | solution.py:30
  202.6 92.8 %collective-permute-start.9 = (f32[99,512]{1,0:T(8,128)S(1)}, f32[99,512]{1,0:T(8,128)S(1)}, u32[]{:S(2)}, u32[]{:S(2)}) collective-permute-start(f32[99,512]{1,0:T(8,128)S(1)} %get-tuple-element.6), channel_id=1, source_target_pairs={{128,0},{160,32},{192,64},{224,96},{256,128},{288,160},{320,192},{... | collective-permute-start | bytes 608264 | tf_op jit(solution)/shard_map/ppermute | solution.py:30
  210.5 98.0 %collective-permute-start.7 = (f32[99,512]{1,0:T(8,128)S(1)}, f32[99,512]{1,0:T(8,128)S(1)}, u32[]{:S(2)}, u32[]{:S(2)}) collective-permute-start(f32[99,512]{1,0:T(8,128)S(1)} %get-tuple-element.7), channel_id=1, source_target_pairs={{96,0},{128,32},{160,64},{192,96},{224,128},{256,160},{288,192},{3... | collective-permute-start | bytes 608264 | tf_op jit(solution)/shard_map/ppermute | solution.py:30
  238.3 77.9 %collective-permute-start.5 = (f32[99,512]{1,0:T(8,128)S(1)}, f32[99,512]{1,0:T(8,128)S(1)}, u32[]{:S(2)}, u32[]{:S(2)}) collective-permute-start(f32[99,512]{1,0:T(8,128)S(1)} %get-tuple-element.8), channel_id=1, source_target_pairs={{64,0},{96,32},{128,64},{160,96},{192,128},{224,160},{256,192},{28... | collective-permute-start | bytes 608264 | tf_op jit(solution)/shard_map/ppermute | solution.py:30
  260.9 59.7 %collective-permute-start.3 = (f32[99,512]{1,0:T(8,128)S(1)}, f32[99,512]{1,0:T(8,128)S(1)}, u32[]{:S(2)}, u32[]{:S(2)}) collective-permute-start(f32[99,512]{1,0:T(8,128)S(1)} %get-tuple-element.9), channel_id=1, source_target_pairs={{32,0},{64,32},{96,64},{128,96},{160,128},{192,160},{224,192},{256... | collective-permute-start | bytes 608264 | tf_op jit(solution)/shard_map/ppermute | solution.py:30
  329.8 111.3 %collective-permute-start.17 = (f32[32,1024]{1,0:T(8,128)S(1)}, f32[32,1024]{1,0:T(8,128)S(1)}, u32[]{:S(2)}, u32[]{:S(2)}) collective-permute-start(f32[32,1024]{1,0:T(8,128)S(1)} %get-tuple-element.10), channel_id=1, source_target_pairs={{1,0},{2,1},{3,2},{4,3},{5,4},{6,5},{7,6},{8,7},{9,8},{10,9},{11,1... | collective-permute-start | bytes 393224 | tf_op jit(solution)/shard_map/ppermute | solution.py:36
  335.2 105.9 %collective-permute-start.18 = (f32[32,1024]{1,0:T(8,128)S(1)}, f32[32,1024]{1,0:T(8,128)S(1)}, u32[]{:S(2)}, u32[]{:S(2)}) collective-permute-start(f32[32,1024]{1,0:T(8,128)S(1)} %get-tuple-element.11), channel_id=1, source_target_pairs={{0,1},{1,2},{2,3},{3,4},{4,5},{5,6},{6,7},{7,8},{8,9},{9,10},{10,1... | collective-permute-start | bytes 393224 | tf_op jit(solution)/shard_map/ppermute | solution.py:36
where the time goes:
time: 446 us; the launch traced here: 444 us
  waiting for transfers between devices  181 us (41%)
  starting transfers between devices  126 us (28%)
  blocking collectives  103 us (23%)
  matrix products  28.4 us (6%)
    ppermute x15, waiting for transfers between devices, shifted(): return lax.ppermute(block, axis, route)  181 us
    ppermute x15, starting transfers between devices, shifted(): return lax.ppermute(block, axis, route)  112 us
    psum x1, blocking collectives, shards(): summed_loss = lax.psum(local_loss, ('ens', 'grid'))  103 us
  transfers between devices with their start and end apart: 19, of which 14 were waited for; matrix products, arithmetic and copies ran while one was open for 1% of the time, Pallas kernels for 0%

commit v1 on v0

v1 whole, which is shorter than its diff:
```python
import functools

import jax
import jax.numpy as jnp
from jax import lax
from jax.experimental import pallas as pl
from jax.experimental.pallas import tpu as pltpu
from jax.sharding import PartitionSpec as P

smooth_width = 0.1
LANES = 128
CHUNK = 256
TILE = 512
f32 = jnp.float32
bf16 = jnp.bfloat16
VMEM = pl.BlockSpec(memory_space=pltpu.VMEM)
ANYWHERE = pl.BlockSpec(memory_space=pl.ANY)


def grant(kibibytes):
    return pltpu.CompilerParams(vmem_limit_bytes=kibibytes * 2**10)


def started(pairs_of_refs, sems):
    copies = [
        pltpu.make_async_copy(source, target, sems.at[index])
        for index, (source, target) in enumerate(pairs_of_refs)
    ]
    for copy in copies:
        copy.start()
    return copies


def one_hot_rows(ids_ref, blocks, count, offset=0):
    row_of = lax.broadcasted_iota(jnp.int32, (count, LANES), 0) + offset
    return jnp.concatenate(
        [(row_of == ids_ref[j : j + 1, :]).astype(bf16) for j in blocks], axis=1
    )


def window_offset(nodes):
    return (lax.axis_index("grid") - 1) * nodes


def forward_kernel(
    lower_ref,
    upper_ref,
    dst_any,
    src_any,
    own_any,
    readout_any,
    bias_any,
    w_any,
    embed_any,
    forecast_ref,
    slope_any,
    dst_ref,
    src_ref,
    own_ref,
    readout_ref,
    bias_ref,
    w_ref,
    embed_ref,
    readout_pad,
    bias_pad,
    gather_ref,
    scatter_ref,
    sources,
    slope_ref,
    in_sems,
    w_sems,
    embed_sems,
    out_sems,
):
    channels = w_ref.shape[1]
    edges = gather_ref.shape[0]
    points = embed_ref.shape[0]
    variables = readout_ref.shape[0]
    members_nodes = own_ref.shape[0]
    window = 3 * members_nodes
    cuts = [slice(first, first + CHUNK) for first in range(0, channels, CHUNK)]
    small = started(
        [
            (dst_any, dst_ref),
            (src_any, src_ref),
            (own_any, own_ref),
            (readout_any, readout_ref),
            (bias_any, bias_ref),
        ],
        in_sems,
    )
    embeds = started([(embed_any.at[:, cut], embed_ref.at[:, cut]) for cut in cuts], embed_sems)
    weights = started([(w_any.at[:, cut], w_ref.at[:, cut]) for cut in cuts], w_sems)
    readout_pad[...] = jnp.zeros_like(readout_pad)
    bias_pad[...] = jnp.zeros_like(bias_pad)
    for slot in range(2):
        sources[slot, points + window :, :] = jnp.zeros((LANES - window, CHUNK), bf16)
    for copy in small:
        copy.wait()
    readout_pad[:variables, :] = readout_ref[...]
    bias_pad[:, :variables] = bias_ref[...]
    nodes = jnp.concatenate([lower_ref[...], own_ref[...], upper_ref[...]], axis=0)
    lane = lax.broadcasted_iota(jnp.int32, (LANES, LANES), 1)

    def build_tables(rows):
        blocks = range(rows.start // LANES, rows.stop // LANES)
        scatter_ref[:, rows] = one_hot_rows(dst_ref, blocks, points)
        for j in blocks:
            block = slice(j * LANES, (j + 1) * LANES)
            point = jnp.broadcast_to(dst_ref[j : j + 1, :], (LANES, LANES)).T
            node = jnp.broadcast_to(src_ref[j : j + 1, :], (LANES, LANES)).T
            node = node - window_offset(members_nodes)
            for first in range(0, points, LANES):
                gather_ref[block, first : first + LANES] = (lane + first == point).astype(bf16)
            gather_ref[block, points:] = (lane == node).astype(bf16)

    steps = [(n, slice(t, t + TILE)) for n in range(len(cuts)) for t in range(0, edges, TILE)]

    def preact_of(step):
        n, rows = step
        if rows.start == 0:
            embeds[n].wait()
            weights[n].wait()
            proj = jnp.dot(nodes, w_ref[:, cuts[n]], preferred_element_type=f32)
            sources[n % 2, :points, :] = embed_ref[:, cuts[n]]
            sources[n % 2, points : points + window, :] = proj.astype(bf16)
        if n == 0:
            build_tables(rows)
        return jnp.dot(gather_ref[rows, :], sources[n % 2], preferred_element_type=f32)

    stores = []
    total = jnp.broadcast_to(bias_pad[...], forecast_ref.shape)
    following = preact_of(steps[0])
    for index, (n, rows) in enumerate(steps):
        preact = following
        if index + 1 < len(steps):
            following = preact_of(steps[index + 1])
        half = 0.5 * preact
        turn = jnp.tanh(half)
        silu = half + half * turn
        slope_ref[rows, cuts[n]] = (0.5 + 0.5 * turn + silu * (0.5 - 0.5 * turn)).astype(bf16)
        part = jnp.dot(scatter_ref[:, rows], silu.astype(bf16), preferred_element_type=f32)
        summed = part if rows.start == 0 else summed + part
        if rows.stop == edges:
            copy = pltpu.make_async_copy(
                slope_ref.at[:, cuts[n]], slope_any.at[:, cuts[n]], out_sems.at[n]
            )
            copy.start()
            stores.append(copy)
            total = total + lax.dot_general(
                summed.astype(bf16),
                readout_pad[:, cuts[n]],
                (((1,), (1,)), ((), ())),
                preferred_element_type=f32,
            )
    forecast_ref[...] = total
    for copy in stores:
        copy.wait()


def forward(lower, upper, dst, src, own, readout, bias, w_src, embed):
    points, channels = embed.shape
    edges = dst.size
    chunks = channels // CHUNK
    held = [(a.shape, a.dtype) for a in (dst, src, own, readout, bias, w_src, embed)]
    held += [((LANES, channels), bf16), ((1, LANES), f32)]
    held += [((edges, points + LANES), bf16), ((points, edges), bf16)]
    held += [((2, points + LANES, CHUNK), bf16), ((edges, channels), bf16)]
    return pl.pallas_call(
        forward_kernel,
        in_specs=[VMEM] * 2 + [ANYWHERE] * 7,
        out_specs=[VMEM, ANYWHERE],
        out_shape=[
            jax.ShapeDtypeStruct((points, LANES), f32),
            jax.ShapeDtypeStruct((edges, channels), bf16),
        ],
        scratch_shapes=[pltpu.VMEM(shape, kind) for shape, kind in held]
        + [pltpu.SemaphoreType.DMA((count,)) for count in (5, chunks, chunks, chunks)],
        compiler_params=grant(55000),
        cost_estimate=pl.CostEstimate(
            flops=4 * edges * points * channels, bytes_accessed=2**23, transcendentals=edges * channels
        ),
        name="forward",
    )(lower, upper, dst, src, own, readout, bias, w_src, embed)


def pair_kernel(variables, forecasts_ref, target_ref, weight_ref, out_ref, grad_ref):
    members, part, _ = forecasts_ref.shape
    step = 8
    loss = jnp.zeros((step, LANES), f32)
    for first in range(0, part, step):
        rows = slice(first, first + step)
        fc = [forecasts_ref[m, rows, :] for m in range(members)]
        target, weight = target_ref[rows, :], weight_ref[rows, :]
        slopes = [jnp.zeros((step, LANES), f32)] * members
        pair = jnp.zeros((step, LANES), f32)
        for m in range(members):
            for k in range(m + 1, members):
                d = fc[m] - fc[k]
                s = d * d + smooth_width * smooth_width
                q = lax.rsqrt(s)
                pair = pair + (s * q - smooth_width)
                slope = d * q
                slopes[m] = slopes[m] + slope
                slopes[k] = slopes[k] - slope
        skill = jnp.zeros((step, LANES), f32)
        for m in range(members):
            d = fc[m] - target
            s = d * d + smooth_width * smooth_width
            q = lax.rsqrt(s)
            skill = skill + (s * q - smooth_width)
            slopes[m] = weight * (d * q - slopes[m] * (1.0 / (members - 1)))
        loss = loss + weight * (skill - pair * (1.0 / (members - 1)))
        for m in range(members):
            grad_ref[m, rows, :] = slopes[m]
    total = jnp.sum(loss, axis=(0, 1), keepdims=True)
    high = total.astype(bf16).astype(f32)
    middle = (total - high).astype(bf16).astype(f32)
    low = total - high - middle
    lane = lax.broadcasted_iota(jnp.int32, (step, LANES), 1)
    row = lax.broadcasted_iota(jnp.int32, (step, LANES), 0)
    note = jnp.where(lane == variables, high, 0.0)
    note = jnp.where(lane == variables + 1, middle, note)
    note = jnp.where(lane == variables + 2, low, note)
    note = jnp.where(row == 0, note, 0.0)
    spare = lane >= variables
    for m in range(members):
        grad_ref[m, :step, :] = jnp.where(spare, note, grad_ref[m, :step, :])
    out_ref[...] = grad_ref[...].astype(bf16)


def pairs(variables, forecasts, target, weight):
    return pl.pallas_call(
        functools.partial(pair_kernel, variables),
        in_specs=[VMEM] * 3,
        out_specs=VMEM,
        out_shape=jax.ShapeDtypeStruct(forecasts.shape, bf16),
        scratch_shapes=[pltpu.VMEM(forecasts.shape, f32)],
        compiler_params=grant(8192),
        cost_estimate=pl.CostEstimate(flops=2**23, bytes_accessed=2**19, transcendentals=2**19),
        name="pairs",
    )(forecasts, target, weight)


def backward_kernel(
    grad_ref,
    dst_any,
    src_any,
    readout_any,
    slope_any,
    lower_ref,
    own_ref,
    upper_ref,
    dst_ref,
    src_ref,
    readout_ref,
    slope_ref,
    readout_pad,
    in_sems,
    slope_sems,
):
    edges, channels = slope_ref.shape
    points = grad_ref.shape[0]
    nodes = own_ref.shape[0]
    variables = readout_ref.shape[0]
    cuts = [slice(first, first + CHUNK) for first in range(0, channels, CHUNK)]
    small = started(
        [(dst_any, dst_ref), (src_any, src_ref), (readout_any, readout_ref)], in_sems
    )
    loads = started([(slope_any.at[:, cut], slope_ref.at[:, cut]) for cut in cuts], slope_sems)
    readout_pad[...] = jnp.zeros_like(readout_pad)
    for copy in small:
        copy.wait()
    readout_pad[:variables, :] = readout_ref[...]
    blocks = range(edges // LANES)
    scatter = one_hot_rows(dst_ref, blocks, points)
    window_table = one_hot_rows(src_ref, blocks, 3 * nodes, window_offset(nodes))
    edge_grad = jnp.dot(grad_ref[...].T, scatter, preferred_element_type=f32).astype(bf16).T
    for n, cut in enumerate(cuts):
        loads[n].wait()
        grad_pre = []
        for first in range(0, edges, TILE):
            rows = slice(first, first + TILE)
            grad_msg = jnp.dot(edge_grad[rows], readout_pad[:, cut], preferred_element_type=f32)
            grad_msg = grad_msg.astype(bf16).astype(f32)
            grad_pre.append((grad_msg * slope_ref[rows, cut].astype(f32)).astype(bf16))
        grad_pre = jnp.concatenate(grad_pre, axis=0)
        window = jnp.dot(window_table, grad_pre, preferred_element_type=f32)
        lower_ref[:, cut] = window[:nodes]
        own_ref[:, cut] = window[nodes : 2 * nodes]
        upper_ref[:, cut] = window[2 * nodes :]


def backward(grad_points, dst, src, readout, slope, nodes):
    edges, channels = slope.shape
    points = grad_points.shape[0]
    held = [(a.shape, a.dtype) for a in (dst, src, readout, slope)] + [((LANES, channels), bf16)]
    return pl.pallas_call(
        backward_kernel,
        in_specs=[VMEM] + [ANYWHERE] * 4,
        out_specs=[VMEM] * 3,
        out_shape=[jax.ShapeDtypeStruct((nodes, channels), f32)] * 3,
        scratch_shapes=[pltpu.VMEM(shape, kind) for shape, kind in held]
        + [pltpu.SemaphoreType.DMA((3,)), pltpu.SemaphoreType.DMA((channels // CHUNK,))],
        compiler_params=grant(53248),
        cost_estimate=pl.CostEstimate(
            flops=2 * edges * points * channels, bytes_accessed=2**22, transcendentals=0
        ),
        name="backward",
    )(grad_points, dst, src, readout, slope)


def shards(
    hidden_mesh_vectors,
    grid_embed,
    w_src,
    readout_matrix,
    b_out,
    verifying_reanalysis,
    var_w,
    area_w,
    edge_src,
    edge_dst,
):
    nodes_dev = hidden_mesh_vectors.shape[1]
    points_dev = grid_embed.shape[0]
    variables = readout_matrix.shape[0]
    members = lax.axis_size("ens")
    part = points_dev // members
    lane_pad = LANES - variables
    ens_rank = lax.axis_index("ens")
    ends = lax.axis_size("grid") - 1
    upward = [(i, i + 1) for i in range(ends)]
    downward = [(i + 1, i) for i in range(ends)]

    own = hidden_mesh_vectors[0]
    lower = lax.ppermute(own, "grid", upward)
    upper = lax.ppermute(own, "grid", downward)

    src = edge_src.reshape(-1, LANES)
    dst = edge_dst.reshape(-1, LANES)
    var_weight = jnp.pad(var_w, (0, lane_pad))
    area = lax.dynamic_slice_in_dim(area_w, ens_rank * part, part, axis=0)
    target = lax.dynamic_slice_in_dim(verifying_reanalysis, ens_rank * part, part, axis=1)
    target = jnp.pad(target.T, ((0, 0), (0, lane_pad)))
    weight = area[:, None] * var_weight[None, :]

    forecast, slope = forward(
        lower, upper, dst, src, own, readout_matrix, b_out[None, :], w_src, grid_embed
    )
    forecasts = lax.all_to_all(forecast.reshape(members, part, LANES), "ens", 0, 0)
    grad_members = pairs(variables, forecasts, target, weight)
    grad_points = lax.all_to_all(grad_members, "ens", 0, 0)

    shards_grid = lax.axis_size("grid")
    notes = jnp.sum(grad_points[:, 0, variables : variables + 3].astype(f32))
    sums = lax.all_to_all(jnp.full((shards_grid, 8, LANES), notes, f32), "grid", 0, 0)
    loss = jnp.sum(sums[:, 0, 0]) / (members * variables * points_dev * shards_grid)

    below, middle, above = backward(
        grad_points.reshape(points_dev, LANES), dst, src, readout_matrix, slope, nodes_dev
    )
    from_above = lax.ppermute(below, "grid", downward)
    from_below = lax.ppermute(above, "grid", upward)
    grad_proj = (middle + from_above + from_below).astype(bf16)
    grad_nodes = lax.dot_general(
        grad_proj, w_src, (((1,), (1,)), ((), ())), preferred_element_type=f32
    )
    return (grad_nodes[None], loss)


def solution(mesh):
    in_specs = (
        P("ens", "grid", None),
        P("grid", None),
        P(),
        P(),
        P(),
        P(None, "grid"),
        P(),
        P("grid"),
        P("grid"),
        P("grid"),
    )
    out_specs = (P("ens", "grid", None), P())
    return jax.shard_map(shards, mesh=mesh, in_specs=in_specs, out_specs=out_specs, check_vma=False)
```

time: 446 us -> 108 us (0.24)
  waiting for transfers between devices: 181 us -> 24.5 us
  starting transfers between devices: 126 us -> 36.9 us
  blocking collectives: 103 us -> 20.2 us
  matrix products: 28.4 us -> 1.38 us
  Pallas kernels: 0 us -> 15 us
  local copies, waits for them, and re-layouts: 0.07 us -> 5.16 us
    ppermute x19 -> x4, waiting for transfers between devices: 181 us -> 7.36 us  [the longest x1 5.16 us: shards(): from_below = lax.ppermute(above, 'grid', upward)]
    ppermute x19 -> x4, starting transfers between devices: 126 us -> 14.3 us  [the longest x1 5.75 us: shards(): upper = lax.ppermute(own, 'grid', downward)]
    psum x1 -> x0, blocking collectives: 103 us -> none  [shards(): summed_loss = lax.psum(local_loss, ('ens', 'grid'))]
    dot_general x5 -> x0, matrix products: 27 us -> none  [the longest x1 6.84 us: shards(): jnp.dot(src_table, grad_pre, preferred_element_type=jnp.float32)]
    all_to_all x0 -> x2, starting transfers between devices: none -> 22.5 us  [the longest x1 15.3 us: shards(): lax.all_to_all(forecast.reshape(members, part, LANES), 'ens', 0, 0)]
    all_to_all x0 -> x1, blocking collectives: none -> 20.2 us  [shards(): grad_points = lax.all_to_all(grad_members, 'ens', 0, 0)]
    all_to_all x0 -> x2, waiting for transfers between devices: none -> 17.1 us  [the longest x1 17.1 us: shards(): lax.all_to_all(forecast.reshape(members, part, LANES), 'ens', 0, 0)]
    pallas_call x0 -> x3, Pallas kernels: none -> 15 us  [the longest x1 10.1 us: forward(): pl.pallas_call(forward_kernel, in_specs=[VMEM] * 2 + [ANYWHERE] * 7, out_...]
  transfers between devices with their start and end apart: 19 -> 6, of which waited for: 14 -> 4; matrix products, arithmetic and copies ran while one was open for 1% -> 2% of each run, Pallas kernels for 0% -> 4%
where the time goes in v1:
time: 108 us; the launch traced here: 107 us
  starting transfers between devices  36.9 us (34%)
  waiting for transfers between devices  24.5 us (23%)
  blocking collectives  20.2 us (19%)
  Pallas kernels  15 us (14%)
  local copies, waits for them, and re-layouts  5.16 us (5%)
  between operations  2.59 us (2%)
  other arithmetic  1.39 us (1%)
  matrix products  1.38 us (1%)
    all_to_all x1, blocking collectives, shards(): grad_points = lax.all_to_all(grad_members, 'ens', 0, 0)  20.2 us
    all_to_all x1, waiting for transfers between devices, shards(): lax.all_to_all(forecast.reshape(members, part, LANES), 'ens', 0, 0)  17.1 us
    all_to_all x1, starting transfers between devices, shards(): lax.all_to_all(forecast.reshape(members, part, LANES), 'ens', 0, 0)  15.3 us
    pallas_call x1, Pallas kernels, forward(): pl.pallas_call(forward_kernel, in_specs=[VMEM] * 2 + [ANYWHERE] * 7, out_...  10.1 us
    all_to_all x1, starting transfers between devices, shards(): lax.all_to_all(jnp.full((shards_grid, 8, LANES), notes, f32), 'grid', 0, 0)  7.21 us
    ppermute x1, starting transfers between devices, shards(): upper = lax.ppermute(own, 'grid', downward)  5.75 us
    ppermute x1, waiting for transfers between devices, shards(): from_below = lax.ppermute(above, 'grid', upward)  5.16 us
    ppermute x1, starting transfers between devices, shards(): from_above = lax.ppermute(below, 'grid', downward)  4.62 us
  transfers between devices with their start and end apart: 6, of which 4 were waited for; matrix products, arithmetic and copies ran while one was open for 2% of the time, Pallas kernels for 4%

profile of v1, /device:TPU:6, one launch (start us, length us, event | category | flops | bytes accessed | tf_op | source)
XLA Modules:
  0.0 107.1 jit_solution(14645476268050825127)
XLA Ops:
  0.6 0.0 copy-start
  0.6 2.1 %collective-permute-start = (bf16[32,1024]{1,0:T(8,128)(2,1)}, bf16[32,1024]{1,0:T(8,128)(2,1)S(1)}, u32[]{:S(2)}, u32[]{:S(2)}) collective-permute-start(bf16[32,1024]{1,0:T(8,128)(2,1)} %bitcast.11), channel_id=1, source_target_pairs={{0,1},{1,2},{2,3},{3,4},{4,5},{5,6},{6,7},{7,8},{8,9},{9,10},{10,1... | collective-permute-start | bytes 196616 | tf_op jit(solution)/shard_map/ppermute | solution.py:337
  2.7 5.8 %collective-permute-start.1 = (bf16[32,1024]{1,0:T(8,128)(2,1)}, bf16[32,1024]{1,0:T(8,128)(2,1)S(1)}, u32[]{:S(2)}, u32[]{:S(2)}) collective-permute-start(bf16[32,1024]{1,0:T(8,128)(2,1)} %bitcast.12), channel_id=1, source_target_pairs={{1,0},{2,1},{3,2},{4,3},{5,4},{6,5},{7,6},{8,7},{9,8},{10,9},{11,1... | collective-permute-start | bytes 196616 | tf_op jit(solution)/shard_map/ppermute | solution.py:338
  8.5 0.2 collective-permute-done.lower_ref
  8.7 2.0 %collective-permute-done.1.upper_ref = bf16[32,1024]{1,0:T(8,128)(2,1)S(1)} collective-permute-done((bf16[32,1024]{1,0:T(8,128)(2,1)}, bf16[32,1024]{1,0:T(8,128)(2,1)S(1)}, u32[]{:S(2)}, u32[]{:S(2)}) %collective-permute-start.1) | collective-permute-done | bytes 65568 | tf_op jit(solution)/shard_map/ppermute | solution.py:338
  10.7 0.0 copy-start.2
  10.7 0.8 copy-done.2
  11.5 0.0 copy-start.3
  11.5 0.7 copy-done.3
  12.2 0.0 copy-start.5
  12.2 0.7 copy-done.5
  12.9 0.0 copy-start.7
  12.9 0.7 copy-done.7
  13.6 0.0 copy-start.9
  13.6 10.1 %forward.1 = (f32[512,128]{1,0:T(8,128)}, bf16[1536,1024]{1,0:T(8,128)(2,1)}) custom-call(bf16[32,1024]{1,0:T(8,128)(2,1)S(1)} %collective-permute-done.lower_ref, bf16[32,1024]{1,0:T(8,128)(2,1)S(1)} %collective-permute-done.1.upper_ref, s32[12,128]{1,0:T(8,128)S(1)} %bitcast.14, s32[12,128]{1,0:T(8,128)S(1)} %bitcast.16, bf16[32,1024]{1,0:T(8,128)(2,1)S(1)} %bitcast.13, ...), custom_call_target="tpu_custom_call" | custom-call | flops 3221225472 | bytes 8388608 | tf_op jit(solution)/shard_map/forward/pallas_call | solution.py:169
  23.7 0.0 copy-start.1
  23.7 0.0 copy-start.4
  23.7 0.0 copy-start.6
  23.7 15.3 %all-to-all-start = ((f32[16,32,128]{2,1,0:T(8,128)}), f32[16,32,128]{2,1,0:T(8,128)S(1)}, u32[]{:S(2)}, u32[]{:S(2)}) async-start(f32[16,32,128]{2,1,0:T(8,128)} %bitcast.19), calls=%async_computation | async-start | bytes 524288 | tf_op jit(solution)/shard_map/all_to_all | solution.py:351
  39.1 0.0 copy-done
  39.1 0.1 constant_dynamic-slice_fusion
  39.2 0.1 copy.17
  39.2 0.8 dynamic_slice.7
  40.0 0.0 copy-done.9
  40.0 0.1 broadcast_multiply_fusion.weight_ref
  40.1 17.1 %all-to-all-done.forecasts_ref = f32[16,32,128]{2,1,0:T(8,128)S(1)} async-done(((f32[16,32,128]{2,1,0:T(8,128)}), f32[16,32,128]{2,1,0:T(8,128)S(1)}, u32[]{:S(2)}, u32[]{:S(2)}) %all-to-all-start) | async-done | bytes 262176 | tf_op jit(solution)/shard_map/all_to_all | solution.py:351
  57.2 0.9 pairs.1
  58.1 20.2 %all_to_all.15 = bf16[16,32,128]{2,1,0:T(8,128)(2,1)S(1)} all-to-all(bf16[16,32,128]{2,1,0:T(8,128)(2,1)S(1)} %pairs.1), channel_id=1, replica_groups=mesh['ens'=16,'grid'=32] {'ens'}, dimensions={0} | all-to-all | bytes 262144 | tf_op jit(solution)/shard_map/all_to_all | solution.py:353
  78.3 0.7 fusion
  79.0 1.3 %broadcast_in_dim.13 = f32[32,8,128]{2,1,0:T(8,128)} broadcast(f32[]{:T(128)} %fusion), dimensions={} | broadcast | bytes 131076 | tf_op jit(solution)/shard_map/broadcast_in_dim | solution.py:357
  80.3 7.2 %all-to-all-start.2 = ((f32[32,8,128]{2,1,0:T(8,128)}), f32[32,8,128]{2,1,0:T(8,128)S(1)}, u32[]{:S(2)}, u32[]{:S(2)}) async-start(f32[32,8,128]{2,1,0:T(8,128)} %broadcast_in_dim.13), calls=%async_computation.2 | async-start | bytes 262144 | tf_op jit(solution)/shard_map/all_to_all | solution.py:357
  87.5 0.0 copy-done.1
  87.5 0.0 copy-done.4
  87.6 0.0 copy-done.6
  87.6 0.0 copy-start.8
  87.6 4.0 %backward.1 = (f32[32,1024]{1,0:T(8,128)S(1)}, f32[32,1024]{1,0:T(8,128)S(1)}, f32[32,1024]{1,0:T(8,128)S(1)}) custom-call(bf16[512,128]{1,0:T(8,128)(2,1)S(1)} %bitcast.10, s32[12,128]{1,0:T(8,128)S(1)} %bitcast.15, s32[12,128]{1,0:T(8,128)S(1)} %bitcast.17, bf16[99,1024]{1,0:T(8,128)(2,1)S(1)} %copy-done.1, bf16[1536,1024]{1,0:T(8,128)(2,1)} %get-tuple-element.8.slope_any), custom_call_target="tpu_custom_call" | custom-call | flops 1610612736 | bytes 4194304 | tf_op jit(solution)/shard_map/backward/pallas_call | solution.py:298
  91.6 4.6 %collective-permute-start.2 = (f32[32,1024]{1,0:T(8,128)S(1)}, f32[32,1024]{1,0:T(8,128)S(1)}, u32[]{:S(2)}, u32[]{:S(2)}) collective-permute-start(f32[32,1024]{1,0:T(8,128)S(1)} %get-tuple-element.10), channel_id=1, source_target_pairs={{1,0},{2,1},{3,2},{4,3},{5,4},{6,5},{7,6},{8,7},{9,8},{10,9},{11,1... | collective-permute-start | bytes 393224 | tf_op jit(solution)/shard_map/ppermute | solution.py:363
  96.2 1.9 %collective-permute-start.3 = (f32[32,1024]{1,0:T(8,128)S(1)}, f32[32,1024]{1,0:T(8,128)S(1)}, u32[]{:S(2)}, u32[]{:S(2)}) collective-permute-start(f32[32,1024]{1,0:T(8,128)S(1)} %get-tuple-element.11), channel_id=1, source_target_pairs={{0,1},{1,2},{2,3},{3,4},{4,5},{5,6},{6,7},{7,8},{8,9},{9,10},{10,1... | collective-permute-start | bytes 393224 | tf_op jit(solution)/shard_map/ppermute | solution.py:364
  98.1 0.0 all-to-all-done.2
  98.1 0.6 slice_reduce_fusion
  99.4 0.0 collective-permute-done.2
  99.4 5.2 %collective-permute-done.3 = f32[32,1024]{1,0:T(8,128)S(1)} collective-permute-done((f32[32,1024]{1,0:T(8,128)S(1)}, f32[32,1024]{1,0:T(8,128)S(1)}, u32[]{:S(2)}, u32[]{:S(2)}) %collective-permute-start.3) | collective-permute-done | bytes 131104 | tf_op jit(solution)/shard_map/ppermute | solution.py:364
  104.6 0.0 copy-done.8
  104.6 1.4 %convolution_bitcast_fusion = f32[1,32,1024]{2,1,0:T(8,128)} fusion(bf16[1024,1024]{1,0:T(8,128)(2,1)S(1)} %copy-done.8, f32[32,1024]{1,0:T(8,128)S(1)} %collective-permute-done.3, f32[32,1024]{1,0:T(8,128)S(1)} %get-tuple-element.9, f32[32,1024]{1,0:T(8,128)S(1)} %collective-permute-done.2), kind=kOutput, calls=%fused_computation | convolution fusion | flops 67207168 | bytes 2621440 | tf_op jit(solution)/shard_map/dot_general | solution.py:366
  (2 shorter events, 0.0 us)
Async XLA Ops:
  0.6 38.4 %copy-start = (f32[99,512]{1,0:T(8,128)S(1)}, f32[99,512]{1,0:T(8,128)}, u32[]{:S(2)}) copy-start(f32[99,512]{1,0:T(8,128)} %param.15) | copy-start | bytes 608260
  0.6 8.0 %collective-permute-start = (bf16[32,1024]{1,0:T(8,128)(2,1)}, bf16[32,1024]{1,0:T(8,128)(2,1)S(1)}, u32[]{:S(2)}, u32[]{:S(2)}) collective-permute-start(bf16[32,1024]{1,0:T(8,128)(2,1)} %bitcast.11), channel_id=1, source_target_pairs={{0,1},{1,2},{2,3},{3,4},{4,5},{5,6},{6,7},{7,8},{8,9},{9,10},{10,1... | collective-permute-start | bytes 196616 | tf_op jit(solution)/shard_map/ppermute | solution.py:337
  2.7 8.0 %collective-permute-start.1 = (bf16[32,1024]{1,0:T(8,128)(2,1)}, bf16[32,1024]{1,0:T(8,128)(2,1)S(1)}, u32[]{:S(2)}, u32[]{:S(2)}) collective-permute-start(bf16[32,1024]{1,0:T(8,128)(2,1)} %bitcast.12), channel_id=1, source_target_pairs={{1,0},{2,1},{3,2},{4,3},{5,4},{6,5},{7,6},{8,7},{9,8},{10,9},{11,1... | collective-permute-start | bytes 196616 | tf_op jit(solution)/shard_map/ppermute | solution.py:338
  10.7 0.8 copy-start.2
  11.5 0.7 copy-start.3
  12.2 0.7 copy-start.5
  12.9 0.7 copy-start.7
  13.6 26.4 %copy-start.9 = (f32[99]{0:T(128)S(1)}, f32[99]{0:T(128)}, u32[]{:S(2)}) copy-start(f32[99]{0:T(128)} %param.16) | copy-start | bytes 1192
  23.7 63.9 %copy-start.1 = (bf16[99,1024]{1,0:T(8,128)(2,1)S(1)}, bf16[99,1024]{1,0:T(8,128)(2,1)}, u32[]{:S(2)}) copy-start(bf16[99,1024]{1,0:T(8,128)(2,1)} %readout_any.3) | copy-start | bytes 608260
  23.7 63.9 %copy-start.4 = (s32[1536]{0:T(1024)S(1)}, s32[1536]{0:T(1024)}, u32[]{:S(2)}) copy-start(s32[1536]{0:T(1024)} %param.19) | copy-start | bytes 18436
  23.7 63.9 %copy-start.6 = (s32[1536]{0:T(1024)S(1)}, s32[1536]{0:T(1024)}, u32[]{:S(2)}) copy-start(s32[1536]{0:T(1024)} %param.18) | copy-start | bytes 18436
  23.7 33.5 %all-to-all-start = ((f32[16,32,128]{2,1,0:T(8,128)}), f32[16,32,128]{2,1,0:T(8,128)S(1)}, u32[]{:S(2)}, u32[]{:S(2)}) async-start(f32[16,32,128]{2,1,0:T(8,128)} %bitcast.19), calls=%async_computation | async-start | bytes 524288 | tf_op jit(solution)/shard_map/all_to_all | solution.py:351
  80.3 17.8 %all-to-all-start.2 = ((f32[32,8,128]{2,1,0:T(8,128)}), f32[32,8,128]{2,1,0:T(8,128)S(1)}, u32[]{:S(2)}, u32[]{:S(2)}) async-start(f32[32,8,128]{2,1,0:T(8,128)} %broadcast_in_dim.13), calls=%async_computation.2 | async-start | bytes 262144 | tf_op jit(solution)/shard_map/all_to_all | solution.py:357
  87.6 17.0 %copy-start.8 = (bf16[1024,1024]{1,0:T(8,128)(2,1)S(1)}, bf16[1024,1024]{1,0:T(8,128)(2,1)}, u32[]{:S(2)}) copy-start(bf16[1024,1024]{1,0:T(8,128)(2,1)} %w_any.1) | copy-start | bytes 6291460
  91.6 7.9 %collective-permute-start.2 = (f32[32,1024]{1,0:T(8,128)S(1)}, f32[32,1024]{1,0:T(8,128)S(1)}, u32[]{:S(2)}, u32[]{:S(2)}) collective-permute-start(f32[32,1024]{1,0:T(8,128)S(1)} %get-tuple-element.10), channel_id=1, source_target_pairs={{1,0},{2,1},{3,2},{4,3},{5,4},{6,5},{7,6},{8,7},{9,8},{10,9},{11,1... | collective-permute-start | bytes 393224 | tf_op jit(solution)/shard_map/ppermute | solution.py:363
  96.2 8.4 %collective-permute-start.3 = (f32[32,1024]{1,0:T(8,128)S(1)}, f32[32,1024]{1,0:T(8,128)S(1)}, u32[]{:S(2)}, u32[]{:S(2)}) collective-permute-start(f32[32,1024]{1,0:T(8,128)S(1)} %get-tuple-element.11), channel_id=1, source_target_pairs={{0,1},{1,2},{2,3},{3,4},{4,5},{5,6},{6,7},{7,8},{8,9},{9,10},{10,1... | collective-permute-start | bytes 393224 | tf_op jit(solution)/shard_map/ppermute | solution.py:364

commit v2 on v1

--- a/solution.py
+++ b/solution.py
@@ -9,8 +9,10 @@
 
 smooth_width = 0.1
 LANES = 128
-CHUNK = 256
+CHUNK = 512
 TILE = 512
+CODE_STEPS = 1280.0
+CODE_SCALE = 64.0
 f32 = jnp.float32
 bf16 = jnp.bfloat16
 VMEM = pl.BlockSpec(memory_space=pltpu.VMEM)
@@ -40,6 +42,19 @@
 
 def window_offset(nodes):
     return (lax.axis_index("grid") - 1) * nodes
+
+
+def gather_rows(gather_ref, dst_ref, src_ref, blocks, nodes):
+    points = gather_ref.shape[1] - LANES
+    lane = lax.broadcasted_iota(jnp.int32, (LANES, LANES), 1)
+    for j in blocks:
+        block = slice(j * LANES, (j + 1) * LANES)
+        point = jnp.broadcast_to(dst_ref[j : j + 1, :], (LANES, LANES)).T
+        node = jnp.broadcast_to(src_ref[j : j + 1, :], (LANES, LANES)).T
+        node = node - window_offset(nodes)
+        for first in range(0, points, LANES):
+            gather_ref[block, first : first + LANES] = (lane + first == point).astype(bf16)
+        gather_ref[block, points:] = (lane == node).astype(bf16)
 
 
 def forward_kernel(
@@ -53,7 +68,7 @@
     w_any,
     embed_any,
     forecast_ref,
-    slope_any,
+    proj_ref,
     dst_ref,
     src_ref,
     own_ref,
@@ -66,11 +81,9 @@
     gather_ref,
     scatter_ref,
     sources,
-    slope_ref,
     in_sems,
     w_sems,
     embed_sems,
-    out_sems,
 ):
     channels = w_ref.shape[1]
     edges = gather_ref.shape[0]
@@ -100,19 +113,11 @@
     readout_pad[:variables, :] = readout_ref[...]
     bias_pad[:, :variables] = bias_ref[...]
     nodes = jnp.concatenate([lower_ref[...], own_ref[...], upper_ref[...]], axis=0)
-    lane = lax.broadcasted_iota(jnp.int32, (LANES, LANES), 1)
 
     def build_tables(rows):
         blocks = range(rows.start // LANES, rows.stop // LANES)
         scatter_ref[:, rows] = one_hot_rows(dst_ref, blocks, points)
-        for j in blocks:
-            block = slice(j * LANES, (j + 1) * LANES)
-            point = jnp.broadcast_to(dst_ref[j : j + 1, :], (LANES, LANES)).T
-            node = jnp.broadcast_to(src_ref[j : j + 1, :], (LANES, LANES)).T
-            node = node - window_offset(members_nodes)
-            for first in range(0, points, LANES):
-                gather_ref[block, first : first + LANES] = (lane + first == point).astype(bf16)
-            gather_ref[block, points:] = (lane == node).astype(bf16)
+        gather_rows(gather_ref, dst_ref, src_ref, blocks, members_nodes)
 
     steps = [(n, slice(t, t + TILE)) for n in range(len(cuts)) for t in range(0, edges, TILE)]
 
@@ -121,14 +126,14 @@
         if rows.start == 0:
             embeds[n].wait()
             weights[n].wait()
-            proj = jnp.dot(nodes, w_ref[:, cuts[n]], preferred_element_type=f32)
+            proj = jnp.dot(nodes, w_ref[:, cuts[n]], preferred_element_type=f32).astype(bf16)
+            proj_ref[:, cuts[n]] = proj
             sources[n % 2, :points, :] = embed_ref[:, cuts[n]]
-            sources[n % 2, points : points + window, :] = proj.astype(bf16)
+            sources[n % 2, points : points + window, :] = proj
         if n == 0:
             build_tables(rows)
         return jnp.dot(gather_ref[rows, :], sources[n % 2], preferred_element_type=f32)
 
-    stores = []
     total = jnp.broadcast_to(bias_pad[...], forecast_ref.shape)
     following = preact_of(steps[0])
     for index, (n, rows) in enumerate(steps):
@@ -138,24 +143,18 @@
         half = 0.5 * preact
         turn = jnp.tanh(half)
         silu = half + half * turn
-        slope_ref[rows, cuts[n]] = (0.5 + 0.5 * turn + silu * (0.5 - 0.5 * turn)).astype(bf16)
         part = jnp.dot(scatter_ref[:, rows], silu.astype(bf16), preferred_element_type=f32)
         summed = part if rows.start == 0 else summed + part
         if rows.stop == edges:
-            copy = pltpu.make_async_copy(
-                slope_ref.at[:, cuts[n]], slope_any.at[:, cuts[n]], out_sems.at[n]
-            )
-            copy.start()
-            stores.append(copy)
             total = total + lax.dot_general(
                 summed.astype(bf16),
                 readout_pad[:, cuts[n]],
                 (((1,), (1,)), ((), ())),
                 preferred_element_type=f32,
             )
-    forecast_ref[...] = total
-    for copy in stores:
-        copy.wait()
+    codes = jnp.floor(jnp.log(1.0 + jnp.abs(total) * CODE_SCALE) * CODE_STEPS + 0.5)
+    codes = jnp.where(total < 0.0, -codes, codes)
+    forecast_ref[...] = codes.astype(jnp.int32).astype(jnp.int16)
 
 
 def forward(lower, upper, dst, src, own, readout, bias, w_src, embed):
@@ -165,18 +164,18 @@
     held = [(a.shape, a.dtype) for a in (dst, src, own, readout, bias, w_src, embed)]
     held += [((LANES, channels), bf16), ((1, LANES), f32)]
     held += [((edges, points + LANES), bf16), ((points, edges), bf16)]
-    held += [((2, points + LANES, CHUNK), bf16), ((edges, channels), bf16)]
+    held += [((2, points + LANES, CHUNK), bf16)]
     return pl.pallas_call(
         forward_kernel,
         in_specs=[VMEM] * 2 + [ANYWHERE] * 7,
-        out_specs=[VMEM, ANYWHERE],
+        out_specs=[VMEM] * 2,
         out_shape=[
-            jax.ShapeDtypeStruct((points, LANES), f32),
-            jax.ShapeDtypeStruct((edges, channels), bf16),
+            jax.ShapeDtypeStruct((points, LANES), jnp.int16),
+            jax.ShapeDtypeStruct((3 * own.shape[0], channels), bf16),
         ],
         scratch_shapes=[pltpu.VMEM(shape, kind) for shape, kind in held]
-        + [pltpu.SemaphoreType.DMA((count,)) for count in (5, chunks, chunks, chunks)],
-        compiler_params=grant(55000),
+        + [pltpu.SemaphoreType.DMA((count,)) for count in (5, chunks, chunks)],
+        compiler_params=grant(55350),
         cost_estimate=pl.CostEstimate(
             flops=4 * edges * points * channels, bytes_accessed=2**23, transcendentals=edges * channels
         ),
@@ -184,9 +183,23 @@
     )(lower, upper, dst, src, own, readout, bias, w_src, embed)
 
 
-def pair_kernel(variables, forecasts_ref, target_ref, weight_ref, out_ref, grad_ref):
-    members, part, _ = forecasts_ref.shape
+def pair_kernel(
+    variables,
+    codes_ref,
+    target_ref,
+    weight_ref,
+    after_ref,
+    out_ref,
+    forecasts_ref,
+    grad_ref,
+):
+    del after_ref
+    members, part, _ = codes_ref.shape
     step = 8
+    for m in range(members):
+        codes = codes_ref[m].astype(jnp.int32).astype(f32)
+        size = (jnp.exp(jnp.abs(codes) * (1.0 / CODE_STEPS)) - 1.0) * (1.0 / CODE_SCALE)
+        forecasts_ref[m] = jnp.where(codes < 0.0, -size, size)
     loss = jnp.zeros((step, LANES), f32)
     for first in range(0, part, step):
         rows = slice(first, first + step)
@@ -229,85 +242,182 @@
     out_ref[...] = grad_ref[...].astype(bf16)
 
 
-def pairs(variables, forecasts, target, weight):
+def pairs(variables, forecasts, target, weight, after):
     return pl.pallas_call(
         functools.partial(pair_kernel, variables),
-        in_specs=[VMEM] * 3,
+        in_specs=[VMEM] * 3 + [ANYWHERE],
         out_specs=VMEM,
         out_shape=jax.ShapeDtypeStruct(forecasts.shape, bf16),
-        scratch_shapes=[pltpu.VMEM(forecasts.shape, f32)],
+        scratch_shapes=[pltpu.VMEM(forecasts.shape, f32)] * 2,
         compiler_params=grant(8192),
         cost_estimate=pl.CostEstimate(flops=2**23, bytes_accessed=2**19, transcendentals=2**19),
         name="pairs",
-    )(forecasts, target, weight)
+    )(forecasts, target, weight, after)
+
+
+def slope_kernel(
+    proj_ref,
+    dst_ref,
+    src_ref,
+    readout_ref,
+    embed_ref,
+    slope_any,
+    window_ref,
+    readout_pad,
+    gather_ref,
+    sources,
+    slope_ref,
+    sems,
+):
+    edges, channels = slope_ref.shape
+    points = embed_ref.shape[0]
+    window = proj_ref.shape[0]
+    blocks = range(edges // LANES)
+    nodes = window // 3
+    gather_rows(gather_ref, dst_ref, src_ref, blocks, nodes)
+    window_ref[...] = one_hot_rows(src_ref, blocks, window, window_offset(nodes))
+    readout_pad[...] = jnp.zeros_like(readout_pad)
+    readout_pad[: readout_ref.shape[0], :] = readout_ref[...]
+    sources[points + window :, :] = jnp.zeros((LANES - window, CHUNK), bf16)
+    stores = []
+    for n, first_channel in enumerate(range(0, channels, CHUNK)):
+        cut = slice(first_channel, first_channel + CHUNK)
+        sources[:points, :] = embed_ref[:, cut]
+        sources[points : points + window, :] = proj_ref[:, cut]
+        for first in range(0, edges, TILE):
+            rows = slice(first, first + TILE)
+            preact = jnp.dot(gather_ref[rows, :], sources[...], preferred_element_type=f32)
+            half = 0.5 * preact
+            turn = jnp.tanh(half)
+            silu = half + half * turn
+            slope = 0.5 + 0.5 * turn + silu * (0.5 - 0.5 * turn)
+            slope_ref[rows, cut] = slope.astype(bf16)
+        stores += started([(slope_ref.at[:, cut], slope_any.at[:, cut])], sems.at[n : n + 1])
+    for copy in stores:
+        copy.wait()
+
+
+def slopes(proj, dst, src, readout, embed):
+    points, channels = embed.shape
+    edges = dst.size
+    return pl.pallas_call(
+        slope_kernel,
+        in_specs=[VMEM] * 5,
+        out_specs=[ANYWHERE, VMEM, VMEM],
+        out_shape=[
+            jax.ShapeDtypeStruct((edges, channels), bf16),
+            jax.ShapeDtypeStruct((proj.shape[0], edges), bf16),
+            jax.ShapeDtypeStruct((LANES, channels), bf16),
+        ],
+        scratch_shapes=[
+            pltpu.VMEM((edges, points + LANES), bf16),
+            pltpu.VMEM((points + LANES, CHUNK), bf16),
+            pltpu.VMEM((edges, channels), bf16),
+            pltpu.SemaphoreType.DMA((channels // CHUNK,)),
+        ],
+        compiler_params=grant(53248),
+        cost_estimate=pl.CostEstimate(
+            flops=2 * edges * points * channels, bytes_accessed=2**23, transcendentals=edges * channels
+        ),
+        name="slopes",
+    )(proj, dst, src, readout, embed)
 
 
 def backward_kernel(
     grad_ref,
-    dst_any,
-    src_any,
-    readout_any,
+    dst_ref,
+    window_ref,
+    readout_ref,
     slope_any,
     lower_ref,
     own_ref,
     upper_ref,
-    dst_ref,
-    src_ref,
-    readout_ref,
     slope_ref,
-    readout_pad,
-    in_sems,
-    slope_sems,
+    sems,
 ):
     edges, channels = slope_ref.shape
-    points = grad_ref.shape[0]
     nodes = own_ref.shape[0]
-    variables = readout_ref.shape[0]
     cuts = [slice(first, first + CHUNK) for first in range(0, channels, CHUNK)]
-    small = started(
-        [(dst_any, dst_ref), (src_any, src_ref), (readout_any, readout_ref)], in_sems
-    )
-    loads = started([(slope_any.at[:, cut], slope_ref.at[:, cut]) for cut in cuts], slope_sems)
-    readout_pad[...] = jnp.zeros_like(readout_pad)
-    for copy in small:
-        copy.wait()
-    readout_pad[:variables, :] = readout_ref[...]
-    blocks = range(edges // LANES)
-    scatter = one_hot_rows(dst_ref, blocks, points)
-    window_table = one_hot_rows(src_ref, blocks, 3 * nodes, window_offset(nodes))
-    edge_grad = jnp.dot(grad_ref[...].T, scatter, preferred_element_type=f32).astype(bf16).T
+    loads = started([(slope_any.at[:, cut], slope_ref.at[:, cut]) for cut in cuts], sems)
+    scatter = one_hot_rows(dst_ref, range(edges // LANES), grad_ref.shape[0])
+    edge_grad = jnp.dot(grad_ref[...].T, scatter, preferred_element_type=f32)
+    edge_grad = edge_grad.astype(bf16).T
     for n, cut in enumerate(cuts):
         loads[n].wait()
         grad_pre = []
         for first in range(0, edges, TILE):
             rows = slice(first, first + TILE)
-            grad_msg = jnp.dot(edge_grad[rows], readout_pad[:, cut], preferred_element_type=f32)
+            grad_msg = jnp.dot(edge_grad[rows], readout_ref[:, cut], preferred_element_type=f32)
             grad_msg = grad_msg.astype(bf16).astype(f32)
             grad_pre.append((grad_msg * slope_ref[rows, cut].astype(f32)).astype(bf16))
         grad_pre = jnp.concatenate(grad_pre, axis=0)
-        window = jnp.dot(window_table, grad_pre, preferred_element_type=f32)
-        lower_ref[:, cut] = window[:nodes]
+        window = jnp.dot(window_ref[...], grad_pre, preferred_element_type=f32)
+        lower_ref[:, cut] = window[:nodes].astype(bf16)
         own_ref[:, cut] = window[nodes : 2 * nodes]
-        upper_ref[:, cut] = window[2 * nodes :]
-
-
-def backward(grad_points, dst, src, readout, slope, nodes):
+        upper_ref[:, cut] = window[2 * nodes :].astype(bf16)
+
+
+def backward(grad_points, dst, window, readout, slope, nodes):
     edges, channels = slope.shape
     points = grad_points.shape[0]
-    held = [(a.shape, a.dtype) for a in (dst, src, readout, slope)] + [((LANES, channels), bf16)]
     return pl.pallas_call(
         backward_kernel,
-        in_specs=[VMEM] + [ANYWHERE] * 4,
+        in_specs=[VMEM] * 4 + [ANYWHERE],
         out_specs=[VMEM] * 3,
-        out_shape=[jax.ShapeDtypeStruct((nodes, channels), f32)] * 3,
-        scratch_shapes=[pltpu.VMEM(shape, kind) for shape, kind in held]
-        + [pltpu.SemaphoreType.DMA((3,)), pltpu.SemaphoreType.DMA((channels // CHUNK,))],
-        compiler_params=grant(53248),
+        out_shape=[jax.ShapeDtypeStruct((nodes, channels), kind) for kind in (bf16, f32, bf16)],
+        scratch_shapes=[
+            pltpu.VMEM((edges, channels), bf16),
+            pltpu.SemaphoreType.DMA((channels // CHUNK,)),
+        ],
+        compiler_params=grant(53900),
         cost_estimate=pl.CostEstimate(
             flops=2 * edges * points * channels, bytes_accessed=2**22, transcendentals=0
         ),
         name="backward",
-    )(grad_points, dst, src, readout, slope)
+    )(grad_points, dst, window, readout, slope)
+
+
+def note_kernel(variables, grad_ref, notes_ref):
+    rows = grad_ref[:, :16, :].astype(f32)
+    lane = lax.broadcasted_iota(jnp.int32, rows.shape, 2)
+    row = lax.broadcasted_iota(jnp.int32, rows.shape, 1)
+    kept = (row == 0) & (lane >= variables) & (lane < variables + 3)
+    total = jnp.sum(jnp.sum(jnp.where(kept, rows, 0.0), axis=0), axis=(0, 1), keepdims=True)
+    notes_ref[...] = jnp.broadcast_to(total[None], notes_ref.shape)
+
+
+def loss_notes(variables, grad_points, copies):
+    return pl.pallas_call(
+        functools.partial(note_kernel, variables),
+        in_specs=[VMEM],
+        out_specs=VMEM,
+        out_shape=jax.ShapeDtypeStruct((copies, 8, LANES), f32),
+        compiler_params=grant(4096),
+        name="loss_notes",
+    )(grad_points)
+
+
+def finish_kernel(scale, own_ref, above_ref, below_ref, w_ref, notes_ref, grad_ref, loss_ref):
+    total = own_ref[...] + above_ref[...].astype(f32) + below_ref[...].astype(f32)
+    grad_ref[...] = lax.dot_general(
+        total.astype(bf16), w_ref[...], (((1,), (1,)), ((), ())), preferred_element_type=f32
+    )
+    loss_ref[...] = jnp.sum(notes_ref[...], axis=0)[:1, :1] * scale
+
+
+def finish(scale, own, above, below, w_src, notes):
+    return pl.pallas_call(
+        functools.partial(finish_kernel, scale),
+        in_specs=[VMEM] * 5,
+        out_specs=[VMEM] * 2,
+        out_shape=[
+            jax.ShapeDtypeStruct((own.shape[0], w_src.shape[0]), f32),
+            jax.ShapeDtypeStruct((1, 1), f32),
+        ],
+        compiler_params=grant(8192),
+        cost_estimate=pl.CostEstimate(flops=2**26, bytes_accessed=2**21, transcendentals=0),
+        name="finish",
+    )(own, above, below, w_src, notes)
 
 
 def shards(
@@ -345,28 +455,25 @@
     target = jnp.pad(target.T, ((0, 0), (0, lane_pad)))
     weight = area[:, None] * var_weight[None, :]
 
-    forecast, slope = forward(
+    forecast, proj = forward(
         lower, upper, dst, src, own, readout_matrix, b_out[None, :], w_src, grid_embed
     )
     forecasts = lax.all_to_all(forecast.reshape(members, part, LANES), "ens", 0, 0)
-    grad_members = pairs(variables, forecasts, target, weight)
+    slope, window, readout = slopes(proj, dst, src, readout_matrix, grid_embed)
+    grad_members = pairs(variables, forecasts, target, weight, window)
     grad_points = lax.all_to_all(grad_members, "ens", 0, 0)
 
     shards_grid = lax.axis_size("grid")
-    notes = jnp.sum(grad_points[:, 0, variables : variables + 3].astype(f32))
-    sums = lax.all_to_all(jnp.full((shards_grid, 8, LANES), notes, f32), "grid", 0, 0)
-    loss = jnp.sum(sums[:, 0, 0]) / (members * variables * points_dev * shards_grid)
-
+    notes = loss_notes(variables, grad_points, shards_grid)
+    notes = lax.all_to_all(notes, "grid", 0, 0)
     below, middle, above = backward(
-        grad_points.reshape(points_dev, LANES), dst, src, readout_matrix, slope, nodes_dev
+        grad_points.reshape(points_dev, LANES), dst, window, readout, slope, nodes_dev
     )
     from_above = lax.ppermute(below, "grid", downward)
     from_below = lax.ppermute(above, "grid", upward)
-    grad_proj = (middle + from_above + from_below).astype(bf16)
-    grad_nodes = lax.dot_general(
-        grad_proj, w_src, (((1,), (1,)), ((), ())), preferred_element_type=f32
-    )
-    return (grad_nodes[None], loss)
+    scale = 1.0 / (members * variables * points_dev * shards_grid)
+    grad_nodes, loss = finish(scale, middle, from_above, from_below, w_src, notes)
+    return (grad_nodes[None], loss[0, 0])
 
 
 def solution(mesh):

time: 108 us -> 95.3 us (0.88)
  waiting for transfers between devices: 24.5 us -> 17.6 us
  Pallas kernels: 15 us -> 21.3 us
  starting transfers between devices: 36.9 us -> 33.5 us
  local copies, waits for them, and re-layouts: 5.16 us -> 2.49 us
  between operations: 2.59 us -> 0.79 us
  matrix products: 1.38 us -> 0 us
  other arithmetic: 1.39 us -> 0.07 us
  blocking collectives: 20.2 us -> 19 us
    all_to_all x1, waiting for transfers between devices: 17.1 us -> 5.89 us  [shards(): lax.all_to_all(forecast.reshape(members, part, LANES), 'ens', 0, 0)]
    pallas_call x1 -> x4, Pallas kernels: 3.98 us -> 11.1 us  [the longest x1 5.33 us: slopes(): pl.pallas_call(slope_kernel, in_specs=[VMEM] * 5, out_specs=[ANYWHERE, VM...]
    ppermute x1, waiting for transfers between devices: 0.22 us -> 5.7 us  [shards(): lower = lax.ppermute(own, 'grid', upward)]
    all_to_all x1, starting transfers between devices: 7.21 us -> 5.12 us  [shards(): notes = lax.all_to_all(notes, 'grid', 0, 0)]
    ppermute x1, waiting for transfers between devices: 1.98 us -> 0.27 us  [shards(): upper = lax.ppermute(own, 'grid', downward)]
    dot_general x1 -> x0, matrix products: 1.38 us -> none  [shards(): lax.dot_general(grad_proj, w_src, (((1,), (1,)), ((), ())), preferred_ele...]
    unnamed x21, local copies, waits for them, and re-layouts: 2.99 us -> 1.64 us
    reduce_sum x2 -> x0, other arithmetic: 1.32 us -> none  [the longest x1 0.69 us: shards(): notes = jnp.sum(grad_points[:, 0, variables:variables + 3].astype(f32))]
  transfers between devices with their start and end apart: 6 -> 6, of which waited for: 4 -> 4; matrix products, arithmetic and copies ran while one was open for 2% -> 1% of each run, Pallas kernels for 4% -> 9%
where the time goes in v2:
time: 95.3 us; the launch traced here: 94.8 us
  starting transfers between devices  33.5 us (35%)
  Pallas kernels  21.3 us (22%)
  blocking collectives  19 us (20%)
  waiting for transfers between devices  17.6 us (18%)
  local copies, waits for them, and re-layouts  2.49 us (3%)
    all_to_all x1, blocking collectives, shards(): grad_points = lax.all_to_all(grad_members, 'ens', 0, 0)  19 us
    all_to_all x1, starting transfers between devices, shards(): lax.all_to_all(forecast.reshape(members, part, LANES), 'ens', 0, 0)  15.2 us
    pallas_call x1, Pallas kernels, forward(): pl.pallas_call(forward_kernel, in_specs=[VMEM] * 2 + [ANYWHERE] * 7, out_...  9.15 us
    all_to_all x1, waiting for transfers between devices, shards(): lax.all_to_all(forecast.reshape(members, part, LANES), 'ens', 0, 0)  5.89 us
    ppermute x1, waiting for transfers between devices, shards(): from_below = lax.ppermute(above, 'grid', upward)  5.76 us
    ppermute x1, waiting for transfers between devices, shards(): lower = lax.ppermute(own, 'grid', upward)  5.7 us
    pallas_call x1, Pallas kernels, slopes(): pl.pallas_call(slope_kernel, in_specs=[VMEM] * 5, out_specs=[ANYWHERE, VM...  5.33 us
    all_to_all x1, starting transfers between devices, shards(): notes = lax.all_to_all(notes, 'grid', 0, 0)  5.12 us
  transfers between devices with their start and end apart: 6, of which 4 were waited for; matrix products, arithmetic and copies ran while one was open for 1% of the time, Pallas kernels for 9%

profile of v2, /device:TPU:6, one launch (start us, length us, event | category | flops | bytes accessed | tf_op | source)
XLA Modules:
  0.0 94.8 jit_solution(14054813484937905328)
XLA Ops:
  0.6 0.0 copy-start
  0.6 4.8 %collective-permute-start.1 = (bf16[32,1024]{1,0:T(8,128)(2,1)}, bf16[32,1024]{1,0:T(8,128)(2,1)S(1)}, u32[]{:S(2)}, u32[]{:S(2)}) collective-permute-start(bf16[32,1024]{1,0:T(8,128)(2,1)} %bitcast.18), channel_id=1, source_target_pairs={{1,0},{2,1},{3,2},{4,3},{5,4},{6,5},{7,6},{8,7},{9,8},{10,9},{11,1... | collective-permute-start | bytes 196616 | tf_op jit(solution)/shard_map/ppermute | solution.py:448
  5.4 1.9 %collective-permute-start = (bf16[32,1024]{1,0:T(8,128)(2,1)}, bf16[32,1024]{1,0:T(8,128)(2,1)S(1)}, u32[]{:S(2)}, u32[]{:S(2)}) collective-permute-start(bf16[32,1024]{1,0:T(8,128)(2,1)} %bitcast.19), channel_id=1, source_target_pairs={{0,1},{1,2},{2,3},{3,4},{4,5},{5,6},{6,7},{7,8},{8,9},{9,10},{10,1... | collective-permute-start | bytes 196616 | tf_op jit(solution)/shard_map/ppermute | solution.py:447
  7.3 0.3 collective-permute-done.1.upper_ref
  7.6 0.0 copy-start.7
  7.6 5.7 %collective-permute-done.lower_ref = bf16[32,1024]{1,0:T(8,128)(2,1)S(1)} collective-permute-done((bf16[32,1024]{1,0:T(8,128)(2,1)}, bf16[32,1024]{1,0:T(8,128)(2,1)S(1)}, u32[]{:S(2)}, u32[]{:S(2)}) %collective-permute-start) | collective-permute-done | bytes 65568 | tf_op jit(solution)/shard_map/ppermute | solution.py:447
  13.3 0.0 copy-start.8
  13.3 0.0 copy-done.7
  13.3 0.6 copy-done.8
  13.9 0.0 copy-start.9
  13.9 0.0 copy-start.2
  13.9 0.0 copy-start.3
  13.9 0.0 copy-start.4
  13.9 0.0 copy-start.5
  14.0 9.1 %forward.1 = (s16[512,128]{1,0:T(8,128)(2,1)}, bf16[96,1024]{1,0:T(8,128)(2,1)}) custom-call(bf16[32,1024]{1,0:T(8,128)(2,1)} %copy-done.8, bf16[32,1024]{1,0:T(8,128)(2,1)} %copy-done.7, s32[12,128]{1,0:T(8,128)} %bitcast.12, s32[12,128]{1,0:T(8,128)} %bitcast.10, bf16[32,1024]{1,0:T(8,128)(2,1)} %bitcast.20, bf16[99,1024]{1,0:T(8,128)(2,1)} %readout_ref.1, ...), custom_call_target="tpu_custom_call" | custom-call | flops 3221225472 | bytes 8388608 | tf_op jit(solution)/shard_map/forward/pallas_call | solution.py:168
  23.1 15.2 %all-to-all-start = ((s16[16,32,128]{2,1,0:T(8,128)(2,1)}), s16[16,32,128]{2,1,0:T(8,128)(2,1)S(1)}, u32[]{:S(2)}, u32[]{:S(2)}) async-start(s16[16,32,128]{2,1,0:T(8,128)(2,1)} %bitcast.15), calls=%async_computation | async-start | bytes 262144 | tf_op jit(solution)/shard_map/all_to_all | solution.py:461
  38.3 0.8 dynamic_slice.7
  39.1 0.0 copy-done
  39.1 0.1 constant_dynamic-slice_fusion
  39.2 0.1 copy.13
  39.3 0.0 copy-done.9
  39.3 0.1 broadcast_multiply_fusion.weight_ref
  39.4 0.0 copy-done.2
  39.4 0.0 copy-done.3
  39.4 0.0 copy-done.4
  39.4 0.0 copy-done.5
  39.4 0.0 copy-start.6
  39.4 0.9 copy-done.6
  40.3 5.3 %slopes.1 = (bf16[1536,1024]{1,0:T(8,128)(2,1)}, bf16[96,1536]{1,0:T(8,128)(2,1)S(1)}, bf16[128,1024]{1,0:T(8,128)(2,1)S(1)}) custom-call(bf16[96,1024]{1,0:T(8,128)(2,1)S(1)} %copy-done.6, s32[12,128]{1,0:T(8,128)S(1)} %bitcast.13, s32[12,128]{1,0:T(8,128)S(1)} %bitcast.11, bf16[99,1024]{1,0:T(8,128)(2,1)S(1)} %copy-done.3, bf16[512,1024]{1,0:T(8,128)(2,1)S(1)} %copy-done.2), custom_call_target="tpu_custom_call" | custom-call | flops 1610612736 | bytes 8388608 | tf_op jit(solution)/shard_map/slopes/pallas_call | solution.py:303
  45.6 5.9 %all-to-all-done.codes_ref = s16[16,32,128]{2,1,0:T(8,128)(2,1)S(1)} async-done(((s16[16,32,128]{2,1,0:T(8,128)(2,1)}), s16[16,32,128]{2,1,0:T(8,128)(2,1)S(1)}, u32[]{:S(2)}, u32[]{:S(2)}) %all-to-all-start) | async-done | bytes 131104 | tf_op jit(solution)/shard_map/all_to_all | solution.py:461
  51.5 1.0 %pairs.1 = bf16[16,32,128]{2,1,0:T(8,128)(2,1)S(1)} custom-call(s16[16,32,128]{2,1,0:T(8,128)(2,1)S(1)} %all-to-all-done.codes_ref, f32[32,128]{1,0:T(8,128)S(1)} %pad.8.target_ref, f32[32,128]{1,0:T(8,128)S(1)} %broadcast_multiply_fusion.weight_ref, bf16[96,1536]{1,0:T(8,128)(2,1)S(1)} %get-tuple-element.14.after_ref.window_ref), custom_call_target="tpu_custom_call" | custom-call | flops 8388608 | bytes 524288 | tf_op jit(solution)/shard_map/pairs/pallas_call | solution.py:246
  52.5 19.0 %all_to_all.15.grad_ref = bf16[16,32,128]{2,1,0:T(8,128)(2,1)S(1)} all-to-all(bf16[16,32,128]{2,1,0:T(8,128)(2,1)S(1)} %pairs.1), channel_id=1, replica_groups=mesh['ens'=16,'grid'=32] {'ens'}, dimensions={0} | all-to-all | bytes 262144 | tf_op jit(solution)/shard_map/all_to_all | solution.py:464
  71.6 0.8 loss_notes.1
  72.4 0.0 copy-start.1
  72.4 5.1 %all-to-all-start.2 = ((f32[32,8,128]{2,1,0:T(8,128)}), f32[32,8,128]{2,1,0:T(8,128)S(1)}, u32[]{:S(2)}, u32[]{:S(2)}) async-start(f32[32,8,128]{2,1,0:T(8,128)} %loss_notes.1), calls=%async_computation.2 | async-start | bytes 262144 | tf_op jit(solution)/shard_map/all_to_all | solution.py:468
  77.5 3.6 %backward.1 = (bf16[32,1024]{1,0:T(8,128)(2,1)S(1)}, f32[32,1024]{1,0:T(8,128)S(1)}, bf16[32,1024]{1,0:T(8,128)(2,1)S(1)}) custom-call(bf16[512,128]{1,0:T(8,128)(2,1)S(1)} %bitcast.9, s32[12,128]{1,0:T(8,128)S(1)} %bitcast.14, bf16[96,1536]{1,0:T(8,128)(2,1)S(1)} %get-tuple-element.14.after_ref.window_ref, ...), custom_call_target="tpu_custom_call" | custom-call | flops 1610612736 | bytes 4194304 | tf_op jit(solution)/shard_map/backward/pallas_call | solution.py:363
  81.1 4.6 %collective-permute-start.2 = (bf16[32,1024]{1,0:T(8,128)(2,1)S(1)}, bf16[32,1024]{1,0:T(8,128)(2,1)S(1)}, u32[]{:S(2)}, u32[]{:S(2)}) collective-permute-start(bf16[32,1024]{1,0:T(8,128)(2,1)S(1)} %get-tuple-element.18), channel_id=1, source_target_pairs={{1,0},{2,1},{3,2},{4,3},{5,4},{6,5},{7,6},{8,7},{9,8},{10,9},{11,1... | collective-permute-start | bytes 196616 | tf_op jit(solution)/shard_map/ppermute | solution.py:472
  85.7 1.9 %collective-permute-start.3 = (bf16[32,1024]{1,0:T(8,128)(2,1)S(1)}, bf16[32,1024]{1,0:T(8,128)(2,1)S(1)}, u32[]{:S(2)}, u32[]{:S(2)}) collective-permute-start(bf16[32,1024]{1,0:T(8,128)(2,1)S(1)} %get-tuple-element.19), channel_id=1, source_target_pairs={{0,1},{1,2},{2,3},{3,4},{4,5},{5,6},{6,7},{7,8},{8,9},{9,10},{10,1... | collective-permute-start | bytes 196616 | tf_op jit(solution)/shard_map/ppermute | solution.py:473
  87.7 0.0 collective-permute-done.2.above_ref
  87.7 5.8 %collective-permute-done.3.below_ref = bf16[32,1024]{1,0:T(8,128)(2,1)S(1)} collective-permute-done((bf16[32,1024]{1,0:T(8,128)(2,1)S(1)}, bf16[32,1024]{1,0:T(8,128)(2,1)S(1)}, u32[]{:S(2)}, u32[]{:S(2)}) %collective-permute-start.3) | collective-permute-done | bytes 65568 | tf_op jit(solution)/shard_map/ppermute | solution.py:473
  93.4 0.0 all-to-all-done.2.notes_ref
  93.4 0.0 copy-done.1
  93.4 1.4 %finish.1 = (f32[32,1024]{1,0:T(8,128)}, f32[1,1]{1,0:T(1,128)}) custom-call(f32[32,1024]{1,0:T(8,128)S(1)} %get-tuple-element.17.own_ref, bf16[32,1024]{1,0:T(8,128)(2,1)S(1)} %collective-permute-done.2.above_ref, bf16[32,1024]{1,0:T(8,128)(2,1)S(1)} %collective-permute-done.3.below_ref, bf16[1024,1024]{1,0:T(8,128)(2,1)S(1)} %copy-done.1, ...), custom_call_target="tpu_custom_call" | custom-call | flops 67108864 | bytes 2097152 | tf_op jit(solution)/shard_map/finish/pallas_call | solution.py:409
  (2 shorter events, 0.0 us)
Async XLA Ops:
  0.6 38.5 %copy-start = (f32[99,512]{1,0:T(8,128)S(1)}, f32[99,512]{1,0:T(8,128)}, u32[]{:S(2)}) copy-start(f32[99,512]{1,0:T(8,128)} %param.15) | copy-start | bytes 608260
  0.6 7.0 %collective-permute-start.1 = (bf16[32,1024]{1,0:T(8,128)(2,1)}, bf16[32,1024]{1,0:T(8,128)(2,1)S(1)}, u32[]{:S(2)}, u32[]{:S(2)}) collective-permute-start(bf16[32,1024]{1,0:T(8,128)(2,1)} %bitcast.18), channel_id=1, source_target_pairs={{1,0},{2,1},{3,2},{4,3},{5,4},{6,5},{7,6},{8,7},{9,8},{10,9},{11,1... | collective-permute-start | bytes 196616 | tf_op jit(solution)/shard_map/ppermute | solution.py:448
  5.4 7.9 %collective-permute-start = (bf16[32,1024]{1,0:T(8,128)(2,1)}, bf16[32,1024]{1,0:T(8,128)(2,1)S(1)}, u32[]{:S(2)}, u32[]{:S(2)}) collective-permute-start(bf16[32,1024]{1,0:T(8,128)(2,1)} %bitcast.19), channel_id=1, source_target_pairs={{0,1},{1,2},{2,3},{3,4},{4,5},{5,6},{6,7},{7,8},{8,9},{9,10},{10,1... | collective-permute-start | bytes 196616 | tf_op jit(solution)/shard_map/ppermute | solution.py:447
  7.6 5.7 %copy-start.7 = (bf16[32,1024]{1,0:T(8,128)(2,1)}, bf16[32,1024]{1,0:T(8,128)(2,1)S(1)}, u32[]{:S(2)}) copy-start(bf16[32,1024]{1,0:T(8,128)(2,1)S(1)} %collective-permute-done.1.upper_ref) | copy-start | bytes 196612
  13.3 0.6 copy-start.8
  13.9 25.3 %copy-start.9 = (f32[99]{0:T(128)S(1)}, f32[99]{0:T(128)}, u32[]{:S(2)}) copy-start(f32[99]{0:T(128)} %param.16) | copy-start | bytes 1192
  13.9 25.4 %copy-start.2 = (bf16[512,1024]{1,0:T(8,128)(2,1)S(1)}, bf16[512,1024]{1,0:T(8,128)(2,1)}, u32[]{:S(2)}) copy-start(bf16[512,1024]{1,0:T(8,128)(2,1)} %embed_ref.1) | copy-start | bytes 3145732
  13.9 25.4 %copy-start.3 = (bf16[99,1024]{1,0:T(8,128)(2,1)S(1)}, bf16[99,1024]{1,0:T(8,128)(2,1)}, u32[]{:S(2)}) copy-start(bf16[99,1024]{1,0:T(8,128)(2,1)} %readout_ref.1) | copy-start | bytes 608260
  13.9 25.4 %copy-start.4 = (s32[1536]{0:T(1024)S(1)}, s32[1536]{0:T(1024)}, u32[]{:S(2)}) copy-start(s32[1536]{0:T(1024)} %param.18) | copy-start | bytes 18436
  13.9 25.4 %copy-start.5 = (s32[1536]{0:T(1024)S(1)}, s32[1536]{0:T(1024)}, u32[]{:S(2)}) copy-start(s32[1536]{0:T(1024)} %param.19) | copy-start | bytes 18436
  23.1 28.4 %all-to-all-start = ((s16[16,32,128]{2,1,0:T(8,128)(2,1)}), s16[16,32,128]{2,1,0:T(8,128)(2,1)S(1)}, u32[]{:S(2)}, u32[]{:S(2)}) async-start(s16[16,32,128]{2,1,0:T(8,128)(2,1)} %bitcast.15), calls=%async_computation | async-start | bytes 262144 | tf_op jit(solution)/shard_map/all_to_all | solution.py:461
  39.4 0.9 copy-start.6
  72.4 21.1 %copy-start.1 = (bf16[1024,1024]{1,0:T(8,128)(2,1)S(1)}, bf16[1024,1024]{1,0:T(8,128)(2,1)}, u32[]{:S(2)}) copy-start(bf16[1024,1024]{1,0:T(8,128)(2,1)} %w_ref.1) | copy-start | bytes 6291460
  72.4 21.1 %all-to-all-start.2 = ((f32[32,8,128]{2,1,0:T(8,128)}), f32[32,8,128]{2,1,0:T(8,128)S(1)}, u32[]{:S(2)}, u32[]{:S(2)}) async-start(f32[32,8,128]{2,1,0:T(8,128)} %loss_notes.1), calls=%async_computation.2 | async-start | bytes 262144 | tf_op jit(solution)/shard_map/all_to_all | solution.py:468
  81.1 6.5 %collective-permute-start.2 = (bf16[32,1024]{1,0:T(8,128)(2,1)S(1)}, bf16[32,1024]{1,0:T(8,128)(2,1)S(1)}, u32[]{:S(2)}, u32[]{:S(2)}) collective-permute-start(bf16[32,1024]{1,0:T(8,128)(2,1)S(1)} %get-tuple-element.18), channel_id=1, source_target_pairs={{1,0},{2,1},{3,2},{4,3},{5,4},{6,5},{7,6},{8,7},{9,8},{10,9},{11,1... | collective-permute-start | bytes 196616 | tf_op jit(solution)/shard_map/ppermute | solution.py:472
  85.7 7.7 %collective-permute-start.3 = (bf16[32,1024]{1,0:T(8,128)(2,1)S(1)}, bf16[32,1024]{1,0:T(8,128)(2,1)S(1)}, u32[]{:S(2)}, u32[]{:S(2)}) collective-permute-start(bf16[32,1024]{1,0:T(8,128)(2,1)S(1)} %get-tuple-element.19), channel_id=1, source_target_pairs={{0,1},{1,2},{2,3},{3,4},{4,5},{5,6},{6,7},{7,8},{8,9},{9,10},{10,1... | collective-permute-start | bytes 196616 | tf_op jit(solution)/shard_map/ppermute | solution.py:473

commit v3 on v2

--- a/solution.py
+++ b/solution.py
@@ -81,6 +81,7 @@
     gather_ref,
     scatter_ref,
     sources,
+    message,
     in_sems,
     w_sems,
     embed_sems,
@@ -143,9 +144,9 @@
         half = 0.5 * preact
         turn = jnp.tanh(half)
         silu = half + half * turn
-        part = jnp.dot(scatter_ref[:, rows], silu.astype(bf16), preferred_element_type=f32)
-        summed = part if rows.start == 0 else summed + part
+        message[n % 2, rows, :] = silu.astype(bf16)
         if rows.stop == edges:
+            summed = jnp.dot(scatter_ref[...], message[n % 2], preferred_element_type=f32)
             total = total + lax.dot_general(
                 summed.astype(bf16),
                 readout_pad[:, cuts[n]],
@@ -164,7 +165,7 @@
     held = [(a.shape, a.dtype) for a in (dst, src, own, readout, bias, w_src, embed)]
     held += [((LANES, channels), bf16), ((1, LANES), f32)]
     held += [((edges, points + LANES), bf16), ((points, edges), bf16)]
-    held += [((2, points + LANES, CHUNK), bf16)]
+    held += [((2, points + LANES, CHUNK), bf16), ((2, edges, CHUNK), bf16)]
     return pl.pallas_call(
         forward_kernel,
         in_specs=[VMEM] * 2 + [ANYWHERE] * 7,
@@ -397,6 +398,26 @@
     )(grad_points)
 
 
+def relay_kernel(notes_ref, below_any, out_ref, passed_any):
+    del below_any, passed_any
+    out_ref[...] = jnp.broadcast_to(jnp.sum(notes_ref[...], axis=0)[None], out_ref.shape)
+
+
+def relay(notes, below, copies):
+    return pl.pallas_call(
+        relay_kernel,
+        in_specs=[VMEM, ANYWHERE],
+        out_specs=[VMEM, ANYWHERE],
+        out_shape=[
+            jax.ShapeDtypeStruct((copies,) + notes.shape[1:], f32),
+            jax.ShapeDtypeStruct(below.shape, below.dtype),
+        ],
+        input_output_aliases={1: 1},
+        compiler_params=grant(4096),
+        name="relay",
+    )(notes, below)
+
+
 def finish_kernel(scale, own_ref, above_ref, below_ref, w_ref, notes_ref, grad_ref, loss_ref):
     total = own_ref[...] + above_ref[...].astype(f32) + below_ref[...].astype(f32)
     grad_ref[...] = lax.dot_general(
@@ -464,11 +485,16 @@
     grad_points = lax.all_to_all(grad_members, "ens", 0, 0)
 
     shards_grid = lax.axis_size("grid")
-    notes = loss_notes(variables, grad_points, shards_grid)
-    notes = lax.all_to_all(notes, "grid", 0, 0)
+    near = 8
+    rows = [[first + j for j in range(near)] for first in range(0, shards_grid, near)]
+    columns = [list(group) for group in zip(*rows)]
+    notes = loss_notes(variables, grad_points, near)
+    notes = lax.all_to_all(notes, "grid", 0, 0, axis_index_groups=rows)
     below, middle, above = backward(
         grad_points.reshape(points_dev, LANES), dst, window, readout, slope, nodes_dev
     )
+    notes, below = relay(notes, below, shards_grid // near)
+    notes = lax.all_to_all(notes, "grid", 0, 0, axis_index_groups=columns)
     from_above = lax.ppermute(below, "grid", downward)
     from_below = lax.ppermute(above, "grid", upward)
     scale = 1.0 / (members * variables * points_dev * shards_grid)

time: 95.3 us -> 98.1 us (1.029)
  blocking collectives: 19 us -> 26.6 us
  waiting for transfers between devices: 17.6 us -> 11.9 us
    all_to_all x0 -> x1, blocking collectives: none -> 7.6 us  [shards(): notes = lax.all_to_all(notes, 'grid', 0, 0, axis_index_groups=columns)]
    ppermute x1, waiting for transfers between devices: 5.76 us -> 0.01 us  [shards(): from_below = lax.ppermute(above, 'grid', upward)]
    all_to_all x1, starting transfers between devices: 5.12 us -> 3.52 us  [shards(): notes = lax.all_to_all(notes, 'grid', 0, 0, axis_index_groups=rows)]
  transfers between devices with their start and end apart: 6 -> 6, of which waited for: 4 -> 3; matrix products, arithmetic and copies ran while one was open for 1% -> 1% of each run, Pallas kernels for 9% -> 9%
where the time goes in v3:
time: 98.1 us; the launch traced here: 96.7 us
  starting transfers between devices  33.1 us (34%)
  blocking collectives  26.6 us (27%)
  Pallas kernels  21.7 us (22%)
  waiting for transfers between devices  11.9 us (12%)
  local copies, waits for them, and re-layouts  2.5 us (3%)
    all_to_all x1, blocking collectives, shards(): grad_points = lax.all_to_all(grad_members, 'ens', 0, 0)  19 us
    all_to_all x1, starting transfers between devices, shards(): lax.all_to_all(forecast.reshape(members, part, LANES), 'ens', 0, 0)  15.2 us
    pallas_call x1, Pallas kernels, forward(): pl.pallas_call(forward_kernel, in_specs=[VMEM] * 2 + [ANYWHERE] * 7, out_...  9.63 us
    all_to_all x1, blocking collectives, shards(): notes = lax.all_to_all(notes, 'grid', 0, 0, axis_index_groups=columns)  7.6 us
    all_to_all x1, waiting for transfers between devices, shards(): lax.all_to_all(forecast.reshape(members, part, LANES), 'ens', 0, 0)  5.89 us
    ppermute x1, waiting for transfers between devices, shards(): lower = lax.ppermute(own, 'grid', upward)  5.7 us
    ppermute x1, starting transfers between devices, shards(): from_above = lax.ppermute(below, 'grid', downward)  5.54 us
    pallas_call x1, Pallas kernels, slopes(): pl.pallas_call(slope_kernel, in_specs=[VMEM] * 5, out_specs=[ANYWHERE, VM...  5.33 us
  transfers between devices with their start and end apart: 6, of which 3 were waited for; matrix products, arithmetic and copies ran while one was open for 1% of the time, Pallas kernels for 9%

profile of v3, /device:TPU:6, one launch (start us, length us, event | category | flops | bytes accessed | tf_op | source)
XLA Modules:
  0.0 96.7 jit_solution(4325411745014219976)
XLA Ops:
  0.6 0.0 copy-start
  0.6 4.8 %collective-permute-start.1 = (bf16[32,1024]{1,0:T(8,128)(2,1)}, bf16[32,1024]{1,0:T(8,128)(2,1)S(1)}, u32[]{:S(2)}, u32[]{:S(2)}) collective-permute-start(bf16[32,1024]{1,0:T(8,128)(2,1)} %bitcast.18), channel_id=1, source_target_pairs={{1,0},{2,1},{3,2},{4,3},{5,4},{6,5},{7,6},{8,7},{9,8},{10,9},{11,1... | collective-permute-start | bytes 196616 | tf_op jit(solution)/shard_map/ppermute | solution.py:469
  5.4 1.9 %collective-permute-start = (bf16[32,1024]{1,0:T(8,128)(2,1)}, bf16[32,1024]{1,0:T(8,128)(2,1)S(1)}, u32[]{:S(2)}, u32[]{:S(2)}) collective-permute-start(bf16[32,1024]{1,0:T(8,128)(2,1)} %bitcast.19), channel_id=1, source_target_pairs={{0,1},{1,2},{2,3},{3,4},{4,5},{5,6},{6,7},{7,8},{8,9},{9,10},{10,1... | collective-permute-start | bytes 196616 | tf_op jit(solution)/shard_map/ppermute | solution.py:468
  7.3 0.3 collective-permute-done.1.upper_ref
  7.6 0.0 copy-start.7
  7.6 5.7 %collective-permute-done.lower_ref = bf16[32,1024]{1,0:T(8,128)(2,1)S(1)} collective-permute-done((bf16[32,1024]{1,0:T(8,128)(2,1)}, bf16[32,1024]{1,0:T(8,128)(2,1)S(1)}, u32[]{:S(2)}, u32[]{:S(2)}) %collective-permute-start) | collective-permute-done | bytes 65568 | tf_op jit(solution)/shard_map/ppermute | solution.py:468
  13.3 0.0 copy-start.8
  13.3 0.0 copy-done.7
  13.3 0.6 copy-done.8
  13.9 0.0 copy-start.9
  13.9 0.0 copy-start.2
  13.9 0.0 copy-start.3
  13.9 0.0 copy-start.4
  14.0 0.0 copy-start.5
  14.0 9.6 %forward.1 = (s16[512,128]{1,0:T(8,128)(2,1)}, bf16[96,1024]{1,0:T(8,128)(2,1)}) custom-call(bf16[32,1024]{1,0:T(8,128)(2,1)} %copy-done.8, bf16[32,1024]{1,0:T(8,128)(2,1)} %copy-done.7, s32[12,128]{1,0:T(8,128)} %bitcast.12, s32[12,128]{1,0:T(8,128)} %bitcast.10, bf16[32,1024]{1,0:T(8,128)(2,1)} %bitcast.20, bf16[99,1024]{1,0:T(8,128)(2,1)} %readout_ref.1, ...), custom_call_target="tpu_custom_call" | custom-call | flops 3221225472 | bytes 8388608 | tf_op jit(solution)/shard_map/forward/pallas_call | solution.py:169
  23.6 15.2 %all-to-all-start = ((s16[16,32,128]{2,1,0:T(8,128)(2,1)}), s16[16,32,128]{2,1,0:T(8,128)(2,1)S(1)}, u32[]{:S(2)}, u32[]{:S(2)}) async-start(s16[16,32,128]{2,1,0:T(8,128)(2,1)} %bitcast.15), calls=%async_computation | async-start | bytes 262144 | tf_op jit(solution)/shard_map/all_to_all | solution.py:482
  38.8 0.8 dynamic_slice.7
  39.6 0.0 copy-done
  39.6 0.1 constant_dynamic-slice_fusion
  39.7 0.1 copy.14
  39.7 0.0 copy-done.9
  39.8 0.1 broadcast_multiply_fusion.weight_ref
  39.8 0.0 copy-done.2
  39.8 0.0 copy-done.3
  39.8 0.0 copy-done.4
  39.9 0.0 copy-done.5
  39.9 0.0 copy-start.6
  39.9 0.9 copy-done.6
  40.8 5.3 %slopes.1 = (bf16[1536,1024]{1,0:T(8,128)(2,1)}, bf16[96,1536]{1,0:T(8,128)(2,1)S(1)}, bf16[128,1024]{1,0:T(8,128)(2,1)S(1)}) custom-call(bf16[96,1024]{1,0:T(8,128)(2,1)S(1)} %copy-done.6, s32[12,128]{1,0:T(8,128)S(1)} %bitcast.13, s32[12,128]{1,0:T(8,128)S(1)} %bitcast.11, bf16[99,1024]{1,0:T(8,128)(2,1)S(1)} %copy-done.3, bf16[512,1024]{1,0:T(8,128)(2,1)S(1)} %copy-done.2), custom_call_target="tpu_custom_call" | custom-call | flops 1610612736 | bytes 8388608 | tf_op jit(solution)/shard_map/slopes/pallas_call | solution.py:304
  46.1 5.9 %all-to-all-done.codes_ref = s16[16,32,128]{2,1,0:T(8,128)(2,1)S(1)} async-done(((s16[16,32,128]{2,1,0:T(8,128)(2,1)}), s16[16,32,128]{2,1,0:T(8,128)(2,1)S(1)}, u32[]{:S(2)}, u32[]{:S(2)}) %all-to-all-start) | async-done | bytes 131104 | tf_op jit(solution)/shard_map/all_to_all | solution.py:482
  52.0 1.0 %pairs.1 = bf16[16,32,128]{2,1,0:T(8,128)(2,1)S(1)} custom-call(s16[16,32,128]{2,1,0:T(8,128)(2,1)S(1)} %all-to-all-done.codes_ref, f32[32,128]{1,0:T(8,128)S(1)} %pad.8.target_ref, f32[32,128]{1,0:T(8,128)S(1)} %broadcast_multiply_fusion.weight_ref, bf16[96,1536]{1,0:T(8,128)(2,1)S(1)} %get-tuple-element.16.after_ref.window_ref), custom_call_target="tpu_custom_call" | custom-call | flops 8388608 | bytes 524288 | tf_op jit(solution)/shard_map/pairs/pallas_call | solution.py:247
  53.0 19.0 %all_to_all.20.grad_ref = bf16[16,32,128]{2,1,0:T(8,128)(2,1)S(1)} all-to-all(bf16[16,32,128]{2,1,0:T(8,128)(2,1)S(1)} %pairs.1), channel_id=1, replica_groups=mesh['ens'=16,'grid'=32] {'ens'}, dimensions={0} | all-to-all | bytes 262144 | tf_op jit(solution)/shard_map/all_to_all | solution.py:485
  72.0 0.0 copy-start.1
  72.1 0.8 loss_notes.1
  72.8 3.5 %all-to-all-start.2 = ((f32[8,8,128]{2,1,0:T(8,128)}), f32[8,8,128]{2,1,0:T(8,128)S(1)}, u32[]{:S(2)}, u32[]{:S(2)}) async-start(f32[8,8,128]{2,1,0:T(8,128)} %loss_notes.1), calls=%async_computation.2 | async-start | bytes 65536 | tf_op jit(solution)/shard_map/all_to_all | solution.py:492
  76.3 3.6 %backward.1 = (bf16[32,1024]{1,0:T(8,128)(2,1)S(1)}, f32[32,1024]{1,0:T(8,128)S(1)}, bf16[32,1024]{1,0:T(8,128)(2,1)S(1)}) custom-call(bf16[512,128]{1,0:T(8,128)(2,1)S(1)} %bitcast.9, s32[12,128]{1,0:T(8,128)S(1)} %bitcast.14, bf16[96,1536]{1,0:T(8,128)(2,1)S(1)} %get-tuple-element.16.after_ref.window_ref, ...), custom_call_target="tpu_custom_call" | custom-call | flops 1610612736 | bytes 4194304 | tf_op jit(solution)/shard_map/backward/pallas_call | solution.py:364
  79.9 2.1 %collective-permute-start.3 = (bf16[32,1024]{1,0:T(8,128)(2,1)S(1)}, bf16[32,1024]{1,0:T(8,128)(2,1)S(1)}, u32[]{:S(2)}, u32[]{:S(2)}) collective-permute-start(bf16[32,1024]{1,0:T(8,128)(2,1)S(1)} %get-tuple-element.22), channel_id=1, source_target_pairs={{0,1},{1,2},{2,3},{3,4},{4,5},{5,6},{6,7},{7,8},{8,9},{9,10},{10,1... | collective-permute-start | bytes 196616 | tf_op jit(solution)/shard_map/ppermute | solution.py:499
  82.1 0.0 all-to-all-done.2.notes_ref
  82.1 5.5 %collective-permute-start.2 = (bf16[32,1024]{1,0:T(8,128)(2,1)S(1)}, bf16[32,1024]{1,0:T(8,128)(2,1)S(1)}, u32[]{:S(2)}, u32[]{:S(2)}) collective-permute-start(bf16[32,1024]{1,0:T(8,128)(2,1)S(1)} %get-tuple-element.21), channel_id=1, source_target_pairs={{1,0},{2,1},{3,2},{4,3},{5,4},{6,5},{7,6},{8,7},{9,8},{10,9},{11,1... | collective-permute-start | bytes 196616 | tf_op jit(solution)/shard_map/ppermute | solution.py:498
  87.7 7.6 %all_to_all.21.notes_ref = f32[4,8,128]{2,1,0:T(8,128)S(1)} all-to-all(f32[4,8,128]{2,1,0:T(8,128)S(1)} %get-tuple-element.23), channel_id=1, replica_groups={{0,8,16,24},{1,9,17,25},{2,10,18,26},{3,11,19,27},{4,12,20,28},{5,13,21..., dimensions={0} | all-to-all | bytes 32768 | tf_op jit(solution)/shard_map/all_to_all | solution.py:497
  95.3 0.0 collective-permute-done.3.below_ref
  95.3 0.0 collective-permute-done.2.above_ref
  95.3 0.0 copy-done.1
  95.3 1.4 %finish.1 = (f32[32,1024]{1,0:T(8,128)}, f32[1,1]{1,0:T(1,128)}) custom-call(f32[32,1024]{1,0:T(8,128)S(1)} %get-tuple-element.19.own_ref, bf16[32,1024]{1,0:T(8,128)(2,1)S(1)} %collective-permute-done.2.above_ref, bf16[32,1024]{1,0:T(8,128)(2,1)S(1)} %collective-permute-done.3.below_ref, bf16[1024,1024]{1,0:T(8,128)(2,1)S(1)} %copy-done.1, ...), custom_call_target="tpu_custom_call" | custom-call | flops 67108864 | bytes 2097152 | tf_op jit(solution)/shard_map/finish/pallas_call | solution.py:430
  (3 shorter events, 0.0 us)
Async XLA Ops:
  0.6 38.9 %copy-start = (f32[99,512]{1,0:T(8,128)S(1)}, f32[99,512]{1,0:T(8,128)}, u32[]{:S(2)}) copy-start(f32[99,512]{1,0:T(8,128)} %param.15) | copy-start | bytes 608260
  0.6 7.0 %collective-permute-start.1 = (bf16[32,1024]{1,0:T(8,128)(2,1)}, bf16[32,1024]{1,0:T(8,128)(2,1)S(1)}, u32[]{:S(2)}, u32[]{:S(2)}) collective-permute-start(bf16[32,1024]{1,0:T(8,128)(2,1)} %bitcast.18), channel_id=1, source_target_pairs={{1,0},{2,1},{3,2},{4,3},{5,4},{6,5},{7,6},{8,7},{9,8},{10,9},{11,1... | collective-permute-start | bytes 196616 | tf_op jit(solution)/shard_map/ppermute | solution.py:469
  5.4 7.9 %collective-permute-start = (bf16[32,1024]{1,0:T(8,128)(2,1)}, bf16[32,1024]{1,0:T(8,128)(2,1)S(1)}, u32[]{:S(2)}, u32[]{:S(2)}) collective-permute-start(bf16[32,1024]{1,0:T(8,128)(2,1)} %bitcast.19), channel_id=1, source_target_pairs={{0,1},{1,2},{2,3},{3,4},{4,5},{5,6},{6,7},{7,8},{8,9},{9,10},{10,1... | collective-permute-start | bytes 196616 | tf_op jit(solution)/shard_map/ppermute | solution.py:468
  7.6 5.7 %copy-start.7 = (bf16[32,1024]{1,0:T(8,128)(2,1)}, bf16[32,1024]{1,0:T(8,128)(2,1)S(1)}, u32[]{:S(2)}) copy-start(bf16[32,1024]{1,0:T(8,128)(2,1)S(1)} %collective-permute-done.1.upper_ref) | copy-start | bytes 196612
  13.3 0.6 copy-start.8
  13.9 25.8 %copy-start.9 = (f32[99]{0:T(128)S(1)}, f32[99]{0:T(128)}, u32[]{:S(2)}) copy-start(f32[99]{0:T(128)} %param.16) | copy-start | bytes 1192
  13.9 25.9 %copy-start.2 = (bf16[512,1024]{1,0:T(8,128)(2,1)S(1)}, bf16[512,1024]{1,0:T(8,128)(2,1)}, u32[]{:S(2)}) copy-start(bf16[512,1024]{1,0:T(8,128)(2,1)} %embed_ref.1) | copy-start | bytes 3145732
  13.9 25.9 %copy-start.3 = (bf16[99,1024]{1,0:T(8,128)(2,1)S(1)}, bf16[99,1024]{1,0:T(8,128)(2,1)}, u32[]{:S(2)}) copy-start(bf16[99,1024]{1,0:T(8,128)(2,1)} %readout_ref.1) | copy-start | bytes 608260
  13.9 25.9 %copy-start.4 = (s32[1536]{0:T(1024)S(1)}, s32[1536]{0:T(1024)}, u32[]{:S(2)}) copy-start(s32[1536]{0:T(1024)} %param.18) | copy-start | bytes 18436
  14.0 25.9 %copy-start.5 = (s32[1536]{0:T(1024)S(1)}, s32[1536]{0:T(1024)}, u32[]{:S(2)}) copy-start(s32[1536]{0:T(1024)} %param.19) | copy-start | bytes 18436
  23.6 28.4 %all-to-all-start = ((s16[16,32,128]{2,1,0:T(8,128)(2,1)}), s16[16,32,128]{2,1,0:T(8,128)(2,1)S(1)}, u32[]{:S(2)}, u32[]{:S(2)}) async-start(s16[16,32,128]{2,1,0:T(8,128)(2,1)} %bitcast.15), calls=%async_computation | async-start | bytes 262144 | tf_op jit(solution)/shard_map/all_to_all | solution.py:482
  39.9 0.9 copy-start.6
  72.0 23.2 %copy-start.1 = (bf16[1024,1024]{1,0:T(8,128)(2,1)S(1)}, bf16[1024,1024]{1,0:T(8,128)(2,1)}, u32[]{:S(2)}) copy-start(bf16[1024,1024]{1,0:T(8,128)(2,1)} %w_ref.1) | copy-start | bytes 6291460
  72.8 9.3 %all-to-all-start.2 = ((f32[8,8,128]{2,1,0:T(8,128)}), f32[8,8,128]{2,1,0:T(8,128)S(1)}, u32[]{:S(2)}, u32[]{:S(2)}) async-start(f32[8,8,128]{2,1,0:T(8,128)} %loss_notes.1), calls=%async_computation.2 | async-start | bytes 65536 | tf_op jit(solution)/shard_map/all_to_all | solution.py:492
  79.9 15.3 %collective-permute-start.3 = (bf16[32,1024]{1,0:T(8,128)(2,1)S(1)}, bf16[32,1024]{1,0:T(8,128)(2,1)S(1)}, u32[]{:S(2)}, u32[]{:S(2)}) collective-permute-start(bf16[32,1024]{1,0:T(8,128)(2,1)S(1)} %get-tuple-element.22), channel_id=1, source_target_pairs={{0,1},{1,2},{2,3},{3,4},{4,5},{5,6},{6,7},{7,8},{8,9},{9,10},{10,1... | collective-permute-start | bytes 196616 | tf_op jit(solution)/shard_map/ppermute | solution.py:499
  82.1 13.2 %collective-permute-start.2 = (bf16[32,1024]{1,0:T(8,128)(2,1)S(1)}, bf16[32,1024]{1,0:T(8,128)(2,1)S(1)}, u32[]{:S(2)}, u32[]{:S(2)}) collective-permute-start(bf16[32,1024]{1,0:T(8,128)(2,1)S(1)} %get-tuple-element.21), channel_id=1, source_target_pairs={{1,0},{2,1},{3,2},{4,3},{5,4},{6,5},{7,6},{8,7},{9,8},{10,9},{11,1... | collective-permute-start | bytes 196616 | tf_op jit(solution)/shard_map/ppermute | solution.py:498

commit v4 on v2

--- a/solution.py
+++ b/solution.py
@@ -10,7 +10,7 @@
 smooth_width = 0.1
 LANES = 128
 CHUNK = 512
-TILE = 512
+TILE = 768
 CODE_STEPS = 1280.0
 CODE_SCALE = 64.0
 f32 = jnp.float32
@@ -323,7 +323,19 @@
     )(proj, dst, src, readout, embed)
 
 
+def loss_note(variables, grad_ref, part):
+    lane = lax.broadcasted_iota(jnp.int32, (16, LANES), 1)
+    row = lax.broadcasted_iota(jnp.int32, (16, LANES), 0)
+    kept = (row == 0) & (lane >= variables) & (lane < variables + 3)
+    total = jnp.zeros((16, LANES), f32)
+    for first in range(0, grad_ref.shape[0], part):
+        total = total + grad_ref[first : first + 16, :].astype(f32)
+    return jnp.sum(jnp.where(kept, total, 0.0), axis=(0, 1), keepdims=True)
+
+
 def backward_kernel(
+    variables,
+    part,
     grad_ref,
     dst_ref,
     window_ref,
@@ -332,6 +344,7 @@
     lower_ref,
     own_ref,
     upper_ref,
+    notes_ref,
     slope_ref,
     sems,
 ):
@@ -339,6 +352,7 @@
     nodes = own_ref.shape[0]
     cuts = [slice(first, first + CHUNK) for first in range(0, channels, CHUNK)]
     loads = started([(slope_any.at[:, cut], slope_ref.at[:, cut]) for cut in cuts], sems)
+    notes_ref[...] = jnp.broadcast_to(loss_note(variables, grad_ref, part)[None], notes_ref.shape)
     scatter = one_hot_rows(dst_ref, range(edges // LANES), grad_ref.shape[0])
     edge_grad = jnp.dot(grad_ref[...].T, scatter, preferred_element_type=f32)
     edge_grad = edge_grad.astype(bf16).T
@@ -357,14 +371,15 @@
         upper_ref[:, cut] = window[2 * nodes :].astype(bf16)
 
 
-def backward(grad_points, dst, window, readout, slope, nodes):
+def backward(variables, part, copies, grad_points, dst, window, readout, slope, nodes):
     edges, channels = slope.shape
     points = grad_points.shape[0]
     return pl.pallas_call(
-        backward_kernel,
+        functools.partial(backward_kernel, variables, part),
         in_specs=[VMEM] * 4 + [ANYWHERE],
-        out_specs=[VMEM] * 3,
-        out_shape=[jax.ShapeDtypeStruct((nodes, channels), kind) for kind in (bf16, f32, bf16)],
+        out_specs=[VMEM] * 4,
+        out_shape=[jax.ShapeDtypeStruct((nodes, channels), kind) for kind in (bf16, f32, bf16)]
+        + [jax.ShapeDtypeStruct((copies, 8, LANES), f32)],
         scratch_shapes=[
             pltpu.VMEM((edges, channels), bf16),
             pltpu.SemaphoreType.DMA((channels // CHUNK,)),
@@ -375,26 +390,6 @@
         ),
         name="backward",
     )(grad_points, dst, window, readout, slope)
-
-
-def note_kernel(variables, grad_ref, notes_ref):
-    rows = grad_ref[:, :16, :].astype(f32)
-    lane = lax.broadcasted_iota(jnp.int32, rows.shape, 2)
-    row = lax.broadcasted_iota(jnp.int32, rows.shape, 1)
-    kept = (row == 0) & (lane >= variables) & (lane < variables + 3)
-    total = jnp.sum(jnp.sum(jnp.where(kept, rows, 0.0), axis=0), axis=(0, 1), keepdims=True)
-    notes_ref[...] = jnp.broadcast_to(total[None], notes_ref.shape)
-
-
-def loss_notes(variables, grad_points, copies):
-    return pl.pallas_call(
-        functools.partial(note_kernel, variables),
-        in_specs=[VMEM],
-        out_specs=VMEM,
-        out_shape=jax.ShapeDtypeStruct((copies, 8, LANES), f32),
-        compiler_params=grant(4096),
-        name="loss_notes",
-    )(grad_points)
 
 
 def finish_kernel(scale, own_ref, above_ref, below_ref, w_ref, notes_ref, grad_ref, loss_ref):
@@ -464,13 +459,20 @@
     grad_points = lax.all_to_all(grad_members, "ens", 0, 0)
 
     shards_grid = lax.axis_size("grid")
-    notes = loss_notes(variables, grad_points, shards_grid)
-    notes = lax.all_to_all(notes, "grid", 0, 0)
-    below, middle, above = backward(
-        grad_points.reshape(points_dev, LANES), dst, window, readout, slope, nodes_dev
+    below, middle, above, notes = backward(
+        variables,
+        part,
+        shards_grid,
+        grad_points.reshape(points_dev, LANES),
+        dst,
+        window,
+        readout,
+        slope,
+        nodes_dev,
     )
     from_above = lax.ppermute(below, "grid", downward)
     from_below = lax.ppermute(above, "grid", upward)
+    notes = lax.all_to_all(notes, "grid", 0, 0)
     scale = 1.0 / (members * variables * points_dev * shards_grid)
     grad_nodes, loss = finish(scale, middle, from_above, from_below, w_src, notes)
     return (grad_nodes[None], loss[0, 0])

time: 95.3 us -> 95.1 us (level)
    pallas_call x2 -> x1, Pallas kernels: 4.41 us -> 3.73 us  [backward(): pl.pallas_call(functools.partial(backward_kernel, variables, part), in_sp...]
  transfers between devices with their start and end apart: 6 -> 6, of which waited for: 4 -> 4; matrix products, arithmetic and copies ran while one was open for 1% -> 1% of each run, Pallas kernels for 9% -> 6%
where the time goes in v4:
time: 95.1 us; the launch traced here: 94.6 us
  starting transfers between devices  33.4 us (35%)
  Pallas kernels  21.2 us (22%)
  blocking collectives  19.1 us (20%)
  waiting for transfers between devices  17.5 us (18%)
  local copies, waits for them, and re-layouts  2.49 us (3%)
    all_to_all x1, blocking collectives, shards(): grad_points = lax.all_to_all(grad_members, 'ens', 0, 0)  19.1 us
    all_to_all x1, starting transfers between devices, shards(): lax.all_to_all(forecast.reshape(members, part, LANES), 'ens', 0, 0)  15.2 us
    pallas_call x1, Pallas kernels, forward(): pl.pallas_call(forward_kernel, in_specs=[VMEM] * 2 + [ANYWHERE] * 7, out_...  9.69 us
    all_to_all x1, waiting for transfers between devices, shards(): lax.all_to_all(forecast.reshape(members, part, LANES), 'ens', 0, 0)  5.78 us
    ppermute x1, waiting for transfers between devices, shards(): from_below = lax.ppermute(above, 'grid', upward)  5.76 us
    ppermute x1, waiting for transfers between devices, shards(): lower = lax.ppermute(own, 'grid', upward)  5.7 us
    pallas_call x1, Pallas kernels, slopes(): pl.pallas_call(slope_kernel, in_specs=[VMEM] * 5, out_specs=[ANYWHERE, VM...  5.45 us
    all_to_all x1, starting transfers between devices, shards(): notes = lax.all_to_all(notes, 'grid', 0, 0)  4.94 us
  transfers between devices with their start and end apart: 6, of which 4 were waited for; matrix products, arithmetic and copies ran while one was open for 1% of the time, Pallas kernels for 6%

profile of v4, /device:TPU:6, one launch (start us, length us, event | category | flops | bytes accessed | tf_op | source)
XLA Modules:
  0.0 94.6 jit_solution(11212828807081449092)
XLA Ops:
  0.6 0.0 copy-start
  0.6 4.8 %collective-permute-start.1 = (bf16[32,1024]{1,0:T(8,128)(2,1)}, bf16[32,1024]{1,0:T(8,128)(2,1)S(1)}, u32[]{:S(2)}, u32[]{:S(2)}) collective-permute-start(bf16[32,1024]{1,0:T(8,128)(2,1)} %bitcast.18), channel_id=1, source_target_pairs={{1,0},{2,1},{3,2},{4,3},{5,4},{6,5},{7,6},{8,7},{9,8},{10,9},{11,1... | collective-permute-start | bytes 196616 | tf_op jit(solution)/shard_map/ppermute | solution.py:443
  5.4 1.9 %collective-permute-start = (bf16[32,1024]{1,0:T(8,128)(2,1)}, bf16[32,1024]{1,0:T(8,128)(2,1)S(1)}, u32[]{:S(2)}, u32[]{:S(2)}) collective-permute-start(bf16[32,1024]{1,0:T(8,128)(2,1)} %bitcast.19), channel_id=1, source_target_pairs={{0,1},{1,2},{2,3},{3,4},{4,5},{5,6},{6,7},{7,8},{8,9},{9,10},{10,1... | collective-permute-start | bytes 196616 | tf_op jit(solution)/shard_map/ppermute | solution.py:442
  7.3 0.3 collective-permute-done.1.upper_ref
  7.6 0.0 copy-start.7
  7.6 5.7 %collective-permute-done.lower_ref = bf16[32,1024]{1,0:T(8,128)(2,1)S(1)} collective-permute-done((bf16[32,1024]{1,0:T(8,128)(2,1)}, bf16[32,1024]{1,0:T(8,128)(2,1)S(1)}, u32[]{:S(2)}, u32[]{:S(2)}) %collective-permute-start) | collective-permute-done | bytes 65568 | tf_op jit(solution)/shard_map/ppermute | solution.py:442
  13.3 0.0 copy-start.8
  13.3 0.0 copy-done.7
  13.3 0.6 copy-done.8
  13.9 0.0 copy-start.9
  13.9 0.0 copy-start.2
  13.9 0.0 copy-start.3
  13.9 0.0 copy-start.4
  13.9 0.0 copy-start.5
  14.0 9.7 %forward.1 = (s16[512,128]{1,0:T(8,128)(2,1)}, bf16[96,1024]{1,0:T(8,128)(2,1)}) custom-call(bf16[32,1024]{1,0:T(8,128)(2,1)} %copy-done.8, bf16[32,1024]{1,0:T(8,128)(2,1)} %copy-done.7, s32[12,128]{1,0:T(8,128)} %bitcast.12, s32[12,128]{1,0:T(8,128)} %bitcast.10, bf16[32,1024]{1,0:T(8,128)(2,1)} %bitcast.20, bf16[99,1024]{1,0:T(8,128)(2,1)} %readout_ref.1, ...), custom_call_target="tpu_custom_call" | custom-call | flops 3221225472 | bytes 8388608 | tf_op jit(solution)/shard_map/forward/pallas_call | solution.py:168
  23.7 15.2 %all-to-all-start = ((s16[16,32,128]{2,1,0:T(8,128)(2,1)}), s16[16,32,128]{2,1,0:T(8,128)(2,1)S(1)}, u32[]{:S(2)}, u32[]{:S(2)}) async-start(s16[16,32,128]{2,1,0:T(8,128)(2,1)} %bitcast.15), calls=%async_computation | async-start | bytes 262144 | tf_op jit(solution)/shard_map/all_to_all | solution.py:456
  38.9 0.8 dynamic_slice.7
  39.6 0.0 copy-done
  39.6 0.1 constant_dynamic-slice_fusion
  39.7 0.1 copy.13
  39.8 0.0 copy-done.9
  39.8 0.1 broadcast_multiply_fusion.weight_ref
  39.9 0.0 copy-done.2
  39.9 0.0 copy-done.3
  39.9 0.0 copy-done.4
  39.9 0.0 copy-done.5
  39.9 0.0 copy-start.6
  39.9 0.9 copy-done.6
  40.9 5.5 %slopes.1 = (bf16[1536,1024]{1,0:T(8,128)(2,1)}, bf16[96,1536]{1,0:T(8,128)(2,1)S(1)}, bf16[128,1024]{1,0:T(8,128)(2,1)S(1)}) custom-call(bf16[96,1024]{1,0:T(8,128)(2,1)S(1)} %copy-done.6, s32[12,128]{1,0:T(8,128)S(1)} %bitcast.13, s32[12,128]{1,0:T(8,128)S(1)} %bitcast.11, bf16[99,1024]{1,0:T(8,128)(2,1)S(1)} %copy-done.3, bf16[512,1024]{1,0:T(8,128)(2,1)S(1)} %copy-done.2), custom_call_target="tpu_custom_call" | custom-call | flops 1610612736 | bytes 8388608 | tf_op jit(solution)/shard_map/slopes/pallas_call | solution.py:303
  46.3 5.8 %all-to-all-done.codes_ref = s16[16,32,128]{2,1,0:T(8,128)(2,1)S(1)} async-done(((s16[16,32,128]{2,1,0:T(8,128)(2,1)}), s16[16,32,128]{2,1,0:T(8,128)(2,1)S(1)}, u32[]{:S(2)}, u32[]{:S(2)}) %all-to-all-start) | async-done | bytes 131104 | tf_op jit(solution)/shard_map/all_to_all | solution.py:456
  52.1 1.0 %pairs.1 = bf16[16,32,128]{2,1,0:T(8,128)(2,1)S(1)} custom-call(s16[16,32,128]{2,1,0:T(8,128)(2,1)S(1)} %all-to-all-done.codes_ref, f32[32,128]{1,0:T(8,128)S(1)} %pad.8.target_ref, f32[32,128]{1,0:T(8,128)S(1)} %broadcast_multiply_fusion.weight_ref, bf16[96,1536]{1,0:T(8,128)(2,1)S(1)} %get-tuple-element.15.after_ref.window_ref), custom_call_target="tpu_custom_call" | custom-call | flops 8388608 | bytes 524288 | tf_op jit(solution)/shard_map/pairs/pallas_call | solution.py:246
  53.1 19.1 %all_to_all.15 = bf16[16,32,128]{2,1,0:T(8,128)(2,1)S(1)} all-to-all(bf16[16,32,128]{2,1,0:T(8,128)(2,1)S(1)} %pairs.1), channel_id=1, replica_groups=mesh['ens'=16,'grid'=32] {'ens'}, dimensions={0} | all-to-all | bytes 262144 | tf_op jit(solution)/shard_map/all_to_all | solution.py:459
  72.2 0.0 copy-start.1
  72.2 3.7 %backward.1 = (bf16[32,1024]{1,0:T(8,128)(2,1)S(1)}, f32[32,1024]{1,0:T(8,128)S(1)}, bf16[32,1024]{1,0:T(8,128)(2,1)S(1)}, f32[32,8,128]{2,1,0:T(8,128)}) custom-call(bf16[512,128]{1,0:T(8,128)(2,1)S(1)} %bitcast.9, s32[12,128]{1,0:T(8,128)S(1)} %bitcast.14, bf16[96,1536]{1,0:T(8,128)(2,1)S(1)} %get-tuple-element.15.after_ref.window_ref, ...), custom_call_target="tpu_custom_call" | custom-call | flops 1610612736 | bytes 4194304 | tf_op jit(solution)/shard_map/backward/pallas_call | solution.py:377
  76.0 4.9 %all-to-all-start.2 = ((f32[32,8,128]{2,1,0:T(8,128)}), f32[32,8,128]{2,1,0:T(8,128)S(1)}, u32[]{:S(2)}, u32[]{:S(2)}) async-start(f32[32,8,128]{2,1,0:T(8,128)} %get-tuple-element.21), calls=%async_computation.2 | async-start | bytes 262144 | tf_op jit(solution)/shard_map/all_to_all | solution.py:475
  80.9 4.6 %collective-permute-start.2 = (bf16[32,1024]{1,0:T(8,128)(2,1)S(1)}, bf16[32,1024]{1,0:T(8,128)(2,1)S(1)}, u32[]{:S(2)}, u32[]{:S(2)}) collective-permute-start(bf16[32,1024]{1,0:T(8,128)(2,1)S(1)} %get-tuple-element.19), channel_id=1, source_target_pairs={{1,0},{2,1},{3,2},{4,3},{5,4},{6,5},{7,6},{8,7},{9,8},{10,9},{11,1... | collective-permute-start | bytes 196616 | tf_op jit(solution)/shard_map/ppermute | solution.py:473
  85.5 1.9 %collective-permute-start.3 = (bf16[32,1024]{1,0:T(8,128)(2,1)S(1)}, bf16[32,1024]{1,0:T(8,128)(2,1)S(1)}, u32[]{:S(2)}, u32[]{:S(2)}) collective-permute-start(bf16[32,1024]{1,0:T(8,128)(2,1)S(1)} %get-tuple-element.20), channel_id=1, source_target_pairs={{0,1},{1,2},{2,3},{3,4},{4,5},{5,6},{6,7},{7,8},{8,9},{9,10},{10,1... | collective-permute-start | bytes 196616 | tf_op jit(solution)/shard_map/ppermute | solution.py:474
  87.5 0.0 collective-permute-done.2.above_ref
  87.5 5.8 %collective-permute-done.3.below_ref = bf16[32,1024]{1,0:T(8,128)(2,1)S(1)} collective-permute-done((bf16[32,1024]{1,0:T(8,128)(2,1)S(1)}, bf16[32,1024]{1,0:T(8,128)(2,1)S(1)}, u32[]{:S(2)}, u32[]{:S(2)}) %collective-permute-start.3) | collective-permute-done | bytes 65568 | tf_op jit(solution)/shard_map/ppermute | solution.py:474
  93.2 0.0 all-to-all-done.2.notes_ref
  93.2 0.0 copy-done.1
  93.2 1.4 %finish.1 = (f32[32,1024]{1,0:T(8,128)}, f32[1,1]{1,0:T(1,128)}) custom-call(f32[32,1024]{1,0:T(8,128)S(1)} %get-tuple-element.18.own_ref, bf16[32,1024]{1,0:T(8,128)(2,1)S(1)} %collective-permute-done.2.above_ref, bf16[32,1024]{1,0:T(8,128)(2,1)S(1)} %collective-permute-done.3.below_ref, bf16[1024,1024]{1,0:T(8,128)(2,1)S(1)} %copy-done.1, ...), custom_call_target="tpu_custom_call" | custom-call | flops 67108864 | bytes 2097152 | tf_op jit(solution)/shard_map/finish/pallas_call | solution.py:404
  (2 shorter events, 0.0 us)
Async XLA Ops:
  0.6 39.0 %copy-start = (f32[99,512]{1,0:T(8,128)S(1)}, f32[99,512]{1,0:T(8,128)}, u32[]{:S(2)}) copy-start(f32[99,512]{1,0:T(8,128)} %param.15) | copy-start | bytes 608260
  0.6 7.0 %collective-permute-start.1 = (bf16[32,1024]{1,0:T(8,128)(2,1)}, bf16[32,1024]{1,0:T(8,128)(2,1)S(1)}, u32[]{:S(2)}, u32[]{:S(2)}) collective-permute-start(bf16[32,1024]{1,0:T(8,128)(2,1)} %bitcast.18), channel_id=1, source_target_pairs={{1,0},{2,1},{3,2},{4,3},{5,4},{6,5},{7,6},{8,7},{9,8},{10,9},{11,1... | collective-permute-start | bytes 196616 | tf_op jit(solution)/shard_map/ppermute | solution.py:443
  5.4 7.9 %collective-permute-start = (bf16[32,1024]{1,0:T(8,128)(2,1)}, bf16[32,1024]{1,0:T(8,128)(2,1)S(1)}, u32[]{:S(2)}, u32[]{:S(2)}) collective-permute-start(bf16[32,1024]{1,0:T(8,128)(2,1)} %bitcast.19), channel_id=1, source_target_pairs={{0,1},{1,2},{2,3},{3,4},{4,5},{5,6},{6,7},{7,8},{8,9},{9,10},{10,1... | collective-permute-start | bytes 196616 | tf_op jit(solution)/shard_map/ppermute | solution.py:442
  7.6 5.7 %copy-start.7 = (bf16[32,1024]{1,0:T(8,128)(2,1)}, bf16[32,1024]{1,0:T(8,128)(2,1)S(1)}, u32[]{:S(2)}) copy-start(bf16[32,1024]{1,0:T(8,128)(2,1)S(1)} %collective-permute-done.1.upper_ref) | copy-start | bytes 196612
  13.3 0.6 copy-start.8
  13.9 25.9 %copy-start.9 = (f32[99]{0:T(128)S(1)}, f32[99]{0:T(128)}, u32[]{:S(2)}) copy-start(f32[99]{0:T(128)} %param.16) | copy-start | bytes 1192
  13.9 26.0 %copy-start.2 = (bf16[512,1024]{1,0:T(8,128)(2,1)S(1)}, bf16[512,1024]{1,0:T(8,128)(2,1)}, u32[]{:S(2)}) copy-start(bf16[512,1024]{1,0:T(8,128)(2,1)} %embed_ref.1) | copy-start | bytes 3145732
  13.9 26.0 %copy-start.3 = (bf16[99,1024]{1,0:T(8,128)(2,1)S(1)}, bf16[99,1024]{1,0:T(8,128)(2,1)}, u32[]{:S(2)}) copy-start(bf16[99,1024]{1,0:T(8,128)(2,1)} %readout_ref.1) | copy-start | bytes 608260
  13.9 26.0 %copy-start.4 = (s32[1536]{0:T(1024)S(1)}, s32[1536]{0:T(1024)}, u32[]{:S(2)}) copy-start(s32[1536]{0:T(1024)} %param.18) | copy-start | bytes 18436
  13.9 26.0 %copy-start.5 = (s32[1536]{0:T(1024)S(1)}, s32[1536]{0:T(1024)}, u32[]{:S(2)}) copy-start(s32[1536]{0:T(1024)} %param.19) | copy-start | bytes 18436
  23.7 28.4 %all-to-all-start = ((s16[16,32,128]{2,1,0:T(8,128)(2,1)}), s16[16,32,128]{2,1,0:T(8,128)(2,1)S(1)}, u32[]{:S(2)}, u32[]{:S(2)}) async-start(s16[16,32,128]{2,1,0:T(8,128)(2,1)} %bitcast.15), calls=%async_computation | async-start | bytes 262144 | tf_op jit(solution)/shard_map/all_to_all | solution.py:456
  39.9 0.9 copy-start.6
  72.2 21.0 %copy-start.1 = (bf16[1024,1024]{1,0:T(8,128)(2,1)S(1)}, bf16[1024,1024]{1,0:T(8,128)(2,1)}, u32[]{:S(2)}) copy-start(bf16[1024,1024]{1,0:T(8,128)(2,1)} %w_ref.1) | copy-start | bytes 6291460
  76.0 17.3 %all-to-all-start.2 = ((f32[32,8,128]{2,1,0:T(8,128)}), f32[32,8,128]{2,1,0:T(8,128)S(1)}, u32[]{:S(2)}, u32[]{:S(2)}) async-start(f32[32,8,128]{2,1,0:T(8,128)} %get-tuple-element.21), calls=%async_computation.2 | async-start | bytes 262144 | tf_op jit(solution)/shard_map/all_to_all | solution.py:475
  80.9 6.6 %collective-permute-start.2 = (bf16[32,1024]{1,0:T(8,128)(2,1)S(1)}, bf16[32,1024]{1,0:T(8,128)(2,1)S(1)}, u32[]{:S(2)}, u32[]{:S(2)}) collective-permute-start(bf16[32,1024]{1,0:T(8,128)(2,1)S(1)} %get-tuple-element.19), channel_id=1, source_target_pairs={{1,0},{2,1},{3,2},{4,3},{5,4},{6,5},{7,6},{8,7},{9,8},{10,9},{11,1... | collective-permute-start | bytes 196616 | tf_op jit(solution)/shard_map/ppermute | solution.py:473
  85.5 7.7 %collective-permute-start.3 = (bf16[32,1024]{1,0:T(8,128)(2,1)S(1)}, bf16[32,1024]{1,0:T(8,128)(2,1)S(1)}, u32[]{:S(2)}, u32[]{:S(2)}) collective-permute-start(bf16[32,1024]{1,0:T(8,128)(2,1)S(1)} %get-tuple-element.20), channel_id=1, source_target_pairs={{0,1},{1,2},{2,3},{3,4},{4,5},{5,6},{6,7},{7,8},{8,9},{9,10},{10,1... | collective-permute-start | bytes 196616 | tf_op jit(solution)/shard_map/ppermute | solution.py:474

commit v5 on v4

--- a/solution.py
+++ b/solution.py
@@ -10,7 +10,7 @@
 smooth_width = 0.1
 LANES = 128
 CHUNK = 512
-TILE = 768
+TILE = 512
 CODE_STEPS = 1280.0
 CODE_SCALE = 64.0
 f32 = jnp.float32
@@ -352,7 +352,7 @@
     nodes = own_ref.shape[0]
     cuts = [slice(first, first + CHUNK) for first in range(0, channels, CHUNK)]
     loads = started([(slope_any.at[:, cut], slope_ref.at[:, cut]) for cut in cuts], sems)
-    notes_ref[...] = jnp.broadcast_to(loss_note(variables, grad_ref, part)[None], notes_ref.shape)
+    notes_ref[...] = jnp.broadcast_to(loss_note(variables, grad_ref, part), notes_ref.shape)
     scatter = one_hot_rows(dst_ref, range(edges // LANES), grad_ref.shape[0])
     edge_grad = jnp.dot(grad_ref[...].T, scatter, preferred_element_type=f32)
     edge_grad = edge_grad.astype(bf16).T
@@ -371,7 +371,7 @@
         upper_ref[:, cut] = window[2 * nodes :].astype(bf16)
 
 
-def backward(variables, part, copies, grad_points, dst, window, readout, slope, nodes):
+def backward(variables, part, grad_points, dst, window, readout, slope, nodes):
     edges, channels = slope.shape
     points = grad_points.shape[0]
     return pl.pallas_call(
@@ -379,7 +379,7 @@
         in_specs=[VMEM] * 4 + [ANYWHERE],
         out_specs=[VMEM] * 4,
         out_shape=[jax.ShapeDtypeStruct((nodes, channels), kind) for kind in (bf16, f32, bf16)]
-        + [jax.ShapeDtypeStruct((copies, 8, LANES), f32)],
+        + [jax.ShapeDtypeStruct((8, LANES), f32)],
         scratch_shapes=[
             pltpu.VMEM((edges, channels), bf16),
             pltpu.SemaphoreType.DMA((channels // CHUNK,)),
@@ -392,27 +392,54 @@
     )(grad_points, dst, window, readout, slope)
 
 
-def finish_kernel(scale, own_ref, above_ref, below_ref, w_ref, notes_ref, grad_ref, loss_ref):
+def spread_kernel(note_ref, above_ref, below_ref, notes_ref):
+    del above_ref, below_ref
+    notes_ref[...] = jnp.broadcast_to(note_ref[...][None], notes_ref.shape)
+
+
+def spread(note, above, below, copies):
+    return pl.pallas_call(
+        spread_kernel,
+        in_specs=[VMEM, ANYWHERE, ANYWHERE],
+        out_specs=VMEM,
+        out_shape=jax.ShapeDtypeStruct((copies,) + note.shape, f32),
+        compiler_params=grant(4096),
+        name="spread",
+    )(note, above, below)
+
+
+def loss_kernel(scale, notes_ref, loss_ref):
+    loss_ref[...] = jnp.sum(notes_ref[...], axis=0)[:1, :1] * scale
+
+
+def loss_of(scale, notes):
+    return pl.pallas_call(
+        functools.partial(loss_kernel, scale),
+        in_specs=[VMEM],
+        out_specs=VMEM,
+        out_shape=jax.ShapeDtypeStruct((1, 1), f32),
+        compiler_params=grant(4096),
+        name="loss_of",
+    )(notes)
+
+
+def finish_kernel(own_ref, above_ref, below_ref, w_ref, grad_ref):
     total = own_ref[...] + above_ref[...].astype(f32) + below_ref[...].astype(f32)
     grad_ref[...] = lax.dot_general(
         total.astype(bf16), w_ref[...], (((1,), (1,)), ((), ())), preferred_element_type=f32
     )
-    loss_ref[...] = jnp.sum(notes_ref[...], axis=0)[:1, :1] * scale
-
-
-def finish(scale, own, above, below, w_src, notes):
-    return pl.pallas_call(
-        functools.partial(finish_kernel, scale),
-        in_specs=[VMEM] * 5,
-        out_specs=[VMEM] * 2,
-        out_shape=[
-            jax.ShapeDtypeStruct((own.shape[0], w_src.shape[0]), f32),
-            jax.ShapeDtypeStruct((1, 1), f32),
-        ],
+
+
+def finish(own, above, below, w_src):
+    return pl.pallas_call(
+        finish_kernel,
+        in_specs=[VMEM] * 4,
+        out_specs=VMEM,
+        out_shape=jax.ShapeDtypeStruct((own.shape[0], w_src.shape[0]), f32),
         compiler_params=grant(8192),
         cost_estimate=pl.CostEstimate(flops=2**26, bytes_accessed=2**21, transcendentals=0),
         name="finish",
-    )(own, above, below, w_src, notes)
+    )(own, above, below, w_src)
 
 
 def shards(
@@ -462,7 +489,6 @@
     below, middle, above, notes = backward(
         variables,
         part,
-        shards_grid,
         grad_points.reshape(points_dev, LANES),
         dst,
         window,
@@ -472,9 +498,10 @@
     )
     from_above = lax.ppermute(below, "grid", downward)
     from_below = lax.ppermute(above, "grid", upward)
-    notes = lax.all_to_all(notes, "grid", 0, 0)
+    notes = lax.all_to_all(spread(notes, from_above, from_below, shards_grid), "grid", 0, 0)
     scale = 1.0 / (members * variables * points_dev * shards_grid)
-    grad_nodes, loss = finish(scale, middle, from_above, from_below, w_src, notes)
+    grad_nodes = finish(middle, from_above, from_below, w_src)
+    loss = loss_of(scale, notes)
     return (grad_nodes[None], loss[0, 0])
 
 

time: 95.1 us -> 100 us (1.052)
  the two profiles are of different devices: /device:TPU:6 before, /device:TPU:1 now
where the time goes in v5:
time: 100 us; the launch traced here: 99.7 us
  starting transfers between devices  41.2 us (41%)
  Pallas kernels  22 us (22%)
  blocking collectives  18.7 us (19%)
  waiting for transfers between devices  14.5 us (14%)
  local copies, waits for them, and re-layouts  2.51 us (3%)
    all_to_all x1, blocking collectives, shards(): grad_points = lax.all_to_all(grad_members, 'ens', 0, 0)  18.7 us
    all_to_all x1, starting transfers between devices, shards(): lax.all_to_all(spread(notes, from_above, from_below, shards_grid), 'grid'...  11.4 us
    all_to_all x1, starting transfers between devices, shards(): lax.all_to_all(forecast.reshape(members, part, LANES), 'ens', 0, 0)  10.7 us
    pallas_call x1, Pallas kernels, forward(): pl.pallas_call(forward_kernel, in_specs=[VMEM] * 2 + [ANYWHERE] * 7, out_...  9.15 us
    ppermute x1, starting transfers between devices, shards(): upper = lax.ppermute(own, 'grid', downward)  8.92 us
    all_to_all x1, waiting for transfers between devices, shards(): lax.all_to_all(spread(notes, from_above, from_below, shards_grid), 'grid'...  6.31 us
    pallas_call x1, Pallas kernels, slopes(): pl.pallas_call(slope_kernel, in_specs=[VMEM] * 5, out_specs=[ANYWHERE, VM...  5.34 us
    all_to_all x1, waiting for transfers between devices, shards(): lax.all_to_all(forecast.reshape(members, part, LANES), 'ens', 0, 0)  5.28 us
  transfers between devices with their start and end apart: 6, of which 4 were waited for; matrix products, arithmetic and copies ran while one was open for 1% of the time, Pallas kernels for 7%

profile of v5, /device:TPU:1, one launch (start us, length us, event | category | flops | bytes accessed | tf_op | source)
XLA Modules:
  0.0 99.7 jit_solution(10824131538372037719)
XLA Ops:
  0.6 0.0 copy-start
  0.6 8.9 %collective-permute-start.1 = (bf16[32,1024]{1,0:T(8,128)(2,1)}, bf16[32,1024]{1,0:T(8,128)(2,1)S(1)}, u32[]{:S(2)}, u32[]{:S(2)}) collective-permute-start(bf16[32,1024]{1,0:T(8,128)(2,1)} %bitcast.18), channel_id=1, source_target_pairs={{1,0},{2,1},{3,2},{4,3},{5,4},{6,5},{7,6},{8,7},{9,8},{10,9},{11,1... | collective-permute-start | bytes 196616 | tf_op jit(solution)/shard_map/ppermute | solution.py:470
  9.6 1.9 %collective-permute-start = (bf16[32,1024]{1,0:T(8,128)(2,1)}, bf16[32,1024]{1,0:T(8,128)(2,1)S(1)}, u32[]{:S(2)}, u32[]{:S(2)}) collective-permute-start(bf16[32,1024]{1,0:T(8,128)(2,1)} %bitcast.19), channel_id=1, source_target_pairs={{0,1},{1,2},{2,3},{3,4},{4,5},{5,6},{6,7},{7,8},{8,9},{9,10},{10,1... | collective-permute-start | bytes 196616 | tf_op jit(solution)/shard_map/ppermute | solution.py:469
  11.5 0.0 collective-permute-done.1.upper_ref
  11.5 0.0 copy-start.7
  11.5 1.6 %collective-permute-done.lower_ref = bf16[32,1024]{1,0:T(8,128)(2,1)S(1)} collective-permute-done((bf16[32,1024]{1,0:T(8,128)(2,1)}, bf16[32,1024]{1,0:T(8,128)(2,1)S(1)}, u32[]{:S(2)}, u32[]{:S(2)}) %collective-permute-start) | collective-permute-done | bytes 65568 | tf_op jit(solution)/shard_map/ppermute | solution.py:469
  13.1 0.0 copy-start.8
  13.1 0.0 copy-done.7
  13.1 0.6 copy-done.8
  13.8 0.0 copy-start.9
  13.8 0.0 copy-start.2
  13.8 0.0 copy-start.3
  13.8 0.0 copy-start.4
  13.8 0.0 copy-start.5
  13.8 9.2 %forward.1 = (s16[512,128]{1,0:T(8,128)(2,1)}, bf16[96,1024]{1,0:T(8,128)(2,1)}) custom-call(bf16[32,1024]{1,0:T(8,128)(2,1)} %copy-done.8, bf16[32,1024]{1,0:T(8,128)(2,1)} %copy-done.7, s32[12,128]{1,0:T(8,128)} %bitcast.12, s32[12,128]{1,0:T(8,128)} %bitcast.10, bf16[32,1024]{1,0:T(8,128)(2,1)} %bitcast.20, bf16[99,1024]{1,0:T(8,128)(2,1)} %readout_ref.1, ...), custom_call_target="tpu_custom_call" | custom-call | flops 3221225472 | bytes 8388608 | tf_op jit(solution)/shard_map/forward/pallas_call | solution.py:168
  22.9 10.7 %all-to-all-start = ((s16[16,32,128]{2,1,0:T(8,128)(2,1)}), s16[16,32,128]{2,1,0:T(8,128)(2,1)S(1)}, u32[]{:S(2)}, u32[]{:S(2)}) async-start(s16[16,32,128]{2,1,0:T(8,128)(2,1)} %bitcast.16), calls=%async_computation | async-start | bytes 262144 | tf_op jit(solution)/shard_map/all_to_all | solution.py:483
  33.7 0.8 dynamic_slice.7
  34.4 0.0 copy-done
  34.4 0.1 constant_dynamic-slice_fusion
  34.5 0.1 copy.13
  34.6 0.0 copy-done.9
  34.6 0.1 broadcast_multiply_fusion.weight_ref
  34.7 0.0 copy-done.2
  34.7 0.0 copy-done.3
  34.7 0.0 copy-done.4
  34.7 0.0 copy-done.5
  34.7 0.0 copy-start.6
  34.7 0.9 copy-done.6
  35.7 5.3 %slopes.1 = (bf16[1536,1024]{1,0:T(8,128)(2,1)}, bf16[96,1536]{1,0:T(8,128)(2,1)S(1)}, bf16[128,1024]{1,0:T(8,128)(2,1)S(1)}) custom-call(bf16[96,1024]{1,0:T(8,128)(2,1)S(1)} %copy-done.6, s32[12,128]{1,0:T(8,128)S(1)} %bitcast.13, s32[12,128]{1,0:T(8,128)S(1)} %bitcast.11, bf16[99,1024]{1,0:T(8,128)(2,1)S(1)} %copy-done.3, bf16[512,1024]{1,0:T(8,128)(2,1)S(1)} %copy-done.2), custom_call_target="tpu_custom_call" | custom-call | flops 1610612736 | bytes 8388608 | tf_op jit(solution)/shard_map/slopes/pallas_call | solution.py:303
  41.0 5.3 %all-to-all-done.codes_ref = s16[16,32,128]{2,1,0:T(8,128)(2,1)S(1)} async-done(((s16[16,32,128]{2,1,0:T(8,128)(2,1)}), s16[16,32,128]{2,1,0:T(8,128)(2,1)S(1)}, u32[]{:S(2)}, u32[]{:S(2)}) %all-to-all-start) | async-done | bytes 131104 | tf_op jit(solution)/shard_map/all_to_all | solution.py:483
  46.3 1.0 pairs.1
  47.3 18.7 %all_to_all.15 = bf16[16,32,128]{2,1,0:T(8,128)(2,1)S(1)} all-to-all(bf16[16,32,128]{2,1,0:T(8,128)(2,1)S(1)} %pairs.1), channel_id=1, replica_groups=mesh['ens'=16,'grid'=32] {'ens'}, dimensions={0} | all-to-all | bytes 262144 | tf_op jit(solution)/shard_map/all_to_all | solution.py:486
  66.0 0.0 copy-start.1
  66.0 3.9 %backward.1 = (bf16[32,1024]{1,0:T(8,128)(2,1)S(1)}, f32[32,1024]{1,0:T(8,128)S(1)}, bf16[32,1024]{1,0:T(8,128)(2,1)S(1)}, f32[8,128]{1,0:T(8,128)S(1)}) custom-call(bf16[512,128]{1,0:T(8,128)(2,1)S(1)} %bitcast.9, s32[12,128]{1,0:T(8,128)S(1)} %bitcast.14, bf16[96,1536]{1,0:T(8,128)(2,1)S(1)} %get-tuple-element.13.after_ref.window_ref, ...), custom_call_target="tpu_custom_call" | custom-call | flops 1610612736 | bytes 4194304 | tf_op jit(solution)/shard_map/backward/pallas_call | solution.py:377
  69.9 3.2 %collective-permute-start.2 = (bf16[32,1024]{1,0:T(8,128)(2,1)S(1)}, bf16[32,1024]{1,0:T(8,128)(2,1)S(1)}, u32[]{:S(2)}, u32[]{:S(2)}) collective-permute-start(bf16[32,1024]{1,0:T(8,128)(2,1)S(1)} %get-tuple-element.17), channel_id=1, source_target_pairs={{1,0},{2,1},{3,2},{4,3},{5,4},{6,5},{7,6},{8,7},{9,8},{10,9},{11,1... | collective-permute-start | bytes 196616 | tf_op jit(solution)/shard_map/ppermute | solution.py:499
  73.1 5.0 %collective-permute-start.3 = (bf16[32,1024]{1,0:T(8,128)(2,1)S(1)}, bf16[32,1024]{1,0:T(8,128)(2,1)S(1)}, u32[]{:S(2)}, u32[]{:S(2)}) collective-permute-start(bf16[32,1024]{1,0:T(8,128)(2,1)S(1)} %get-tuple-element.18), channel_id=1, source_target_pairs={{0,1},{1,2},{2,3},{3,4},{4,5},{5,6},{6,7},{7,8},{8,9},{9,10},{10,1... | collective-permute-start | bytes 196616 | tf_op jit(solution)/shard_map/ppermute | solution.py:500
  78.1 0.0 collective-permute-done.2.above_ref
  78.1 1.3 %collective-permute-done.3.below_ref = bf16[32,1024]{1,0:T(8,128)(2,1)S(1)} collective-permute-done((bf16[32,1024]{1,0:T(8,128)(2,1)S(1)}, bf16[32,1024]{1,0:T(8,128)(2,1)S(1)}, u32[]{:S(2)}, u32[]{:S(2)}) %collective-permute-start.3) | collective-permute-done | bytes 65568 | tf_op jit(solution)/shard_map/ppermute | solution.py:500
  79.4 0.7 spread.1
  80.1 11.4 %all-to-all-start.2 = ((f32[32,8,128]{2,1,0:T(8,128)}), f32[32,8,128]{2,1,0:T(8,128)S(1)}, u32[]{:S(2)}, u32[]{:S(2)}) async-start(f32[32,8,128]{2,1,0:T(8,128)} %spread.1), calls=%async_computation.2 | async-start | bytes 262144 | tf_op jit(solution)/shard_map/all_to_all | solution.py:501
  91.5 0.0 copy-done.1
  91.5 1.4 %finish.1 = f32[32,1024]{1,0:T(8,128)} custom-call(f32[32,1024]{1,0:T(8,128)S(1)} %get-tuple-element.16.own_ref, bf16[32,1024]{1,0:T(8,128)(2,1)S(1)} %collective-permute-done.2.above_ref, bf16[32,1024]{1,0:T(8,128)(2,1)S(1)} %collective-permute-done.3.below_ref, bf16[1024,1024]{1,0:T(8,128)(2,1)S(1)} %copy-done.1), custom_call_target="tpu_custom_call" | custom-call | flops 67108864 | bytes 2097152 | tf_op jit(solution)/shard_map/finish/pallas_call | solution.py:434
  92.9 6.3 %all-to-all-done.2.notes_ref = f32[32,8,128]{2,1,0:T(8,128)S(1)} async-done(((f32[32,8,128]{2,1,0:T(8,128)}), f32[32,8,128]{2,1,0:T(8,128)S(1)}, u32[]{:S(2)}, u32[]{:S(2)}) %all-to-all-start.2) | async-done | bytes 131104 | tf_op jit(solution)/shard_map/all_to_all | solution.py:501
  99.2 0.5 loss_of.1
  (2 shorter events, 0.0 us)
Async XLA Ops:
  0.6 33.8 %copy-start = (f32[99,512]{1,0:T(8,128)S(1)}, f32[99,512]{1,0:T(8,128)}, u32[]{:S(2)}) copy-start(f32[99,512]{1,0:T(8,128)} %param.15) | copy-start | bytes 608260
  0.6 10.9 %collective-permute-start.1 = (bf16[32,1024]{1,0:T(8,128)(2,1)}, bf16[32,1024]{1,0:T(8,128)(2,1)S(1)}, u32[]{:S(2)}, u32[]{:S(2)}) collective-permute-start(bf16[32,1024]{1,0:T(8,128)(2,1)} %bitcast.18), channel_id=1, source_target_pairs={{1,0},{2,1},{3,2},{4,3},{5,4},{6,5},{7,6},{8,7},{9,8},{10,9},{11,1... | collective-permute-start | bytes 196616 | tf_op jit(solution)/shard_map/ppermute | solution.py:470
  9.6 3.6 %collective-permute-start = (bf16[32,1024]{1,0:T(8,128)(2,1)}, bf16[32,1024]{1,0:T(8,128)(2,1)S(1)}, u32[]{:S(2)}, u32[]{:S(2)}) collective-permute-start(bf16[32,1024]{1,0:T(8,128)(2,1)} %bitcast.19), channel_id=1, source_target_pairs={{0,1},{1,2},{2,3},{3,4},{4,5},{5,6},{6,7},{7,8},{8,9},{9,10},{10,1... | collective-permute-start | bytes 196616 | tf_op jit(solution)/shard_map/ppermute | solution.py:469
  11.5 1.6 %copy-start.7 = (bf16[32,1024]{1,0:T(8,128)(2,1)}, bf16[32,1024]{1,0:T(8,128)(2,1)S(1)}, u32[]{:S(2)}) copy-start(bf16[32,1024]{1,0:T(8,128)(2,1)S(1)} %collective-permute-done.1.upper_ref) | copy-start | bytes 196612
  13.1 0.6 copy-start.8
  13.8 20.8 %copy-start.9 = (f32[99]{0:T(128)S(1)}, f32[99]{0:T(128)}, u32[]{:S(2)}) copy-start(f32[99]{0:T(128)} %param.16) | copy-start | bytes 1192
  13.8 20.9 %copy-start.2 = (bf16[512,1024]{1,0:T(8,128)(2,1)S(1)}, bf16[512,1024]{1,0:T(8,128)(2,1)}, u32[]{:S(2)}) copy-start(bf16[512,1024]{1,0:T(8,128)(2,1)} %embed_ref.1) | copy-start | bytes 3145732
  13.8 20.9 %copy-start.3 = (bf16[99,1024]{1,0:T(8,128)(2,1)S(1)}, bf16[99,1024]{1,0:T(8,128)(2,1)}, u32[]{:S(2)}) copy-start(bf16[99,1024]{1,0:T(8,128)(2,1)} %readout_ref.1) | copy-start | bytes 608260
  13.8 20.9 %copy-start.4 = (s32[1536]{0:T(1024)S(1)}, s32[1536]{0:T(1024)}, u32[]{:S(2)}) copy-start(s32[1536]{0:T(1024)} %param.18) | copy-start | bytes 18436
  13.8 20.9 %copy-start.5 = (s32[1536]{0:T(1024)S(1)}, s32[1536]{0:T(1024)}, u32[]{:S(2)}) copy-start(s32[1536]{0:T(1024)} %param.19) | copy-start | bytes 18436
  22.9 23.3 %all-to-all-start = ((s16[16,32,128]{2,1,0:T(8,128)(2,1)}), s16[16,32,128]{2,1,0:T(8,128)(2,1)S(1)}, u32[]{:S(2)}, u32[]{:S(2)}) async-start(s16[16,32,128]{2,1,0:T(8,128)(2,1)} %bitcast.16), calls=%async_computation | async-start | bytes 262144 | tf_op jit(solution)/shard_map/all_to_all | solution.py:483
  34.7 0.9 copy-start.6
  66.0 25.5 %copy-start.1 = (bf16[1024,1024]{1,0:T(8,128)(2,1)S(1)}, bf16[1024,1024]{1,0:T(8,128)(2,1)}, u32[]{:S(2)}) copy-start(bf16[1024,1024]{1,0:T(8,128)(2,1)} %w_ref.1) | copy-start | bytes 6291460
  69.9 8.3 %collective-permute-start.2 = (bf16[32,1024]{1,0:T(8,128)(2,1)S(1)}, bf16[32,1024]{1,0:T(8,128)(2,1)S(1)}, u32[]{:S(2)}, u32[]{:S(2)}) collective-permute-start(bf16[32,1024]{1,0:T(8,128)(2,1)S(1)} %get-tuple-element.17), channel_id=1, source_target_pairs={{1,0},{2,1},{3,2},{4,3},{5,4},{6,5},{7,6},{8,7},{9,8},{10,9},{11,1... | collective-permute-start | bytes 196616 | tf_op jit(solution)/shard_map/ppermute | solution.py:499
  73.1 6.3 %collective-permute-start.3 = (bf16[32,1024]{1,0:T(8,128)(2,1)S(1)}, bf16[32,1024]{1,0:T(8,128)(2,1)S(1)}, u32[]{:S(2)}, u32[]{:S(2)}) collective-permute-start(bf16[32,1024]{1,0:T(8,128)(2,1)S(1)} %get-tuple-element.18), channel_id=1, source_target_pairs={{0,1},{1,2},{2,3},{3,4},{4,5},{5,6},{6,7},{7,8},{8,9},{9,10},{10,1... | collective-permute-start | bytes 196616 | tf_op jit(solution)/shard_map/ppermute | solution.py:500
  80.1 19.1 %all-to-all-start.2 = ((f32[32,8,128]{2,1,0:T(8,128)}), f32[32,8,128]{2,1,0:T(8,128)S(1)}, u32[]{:S(2)}, u32[]{:S(2)}) async-start(f32[32,8,128]{2,1,0:T(8,128)} %spread.1), calls=%async_computation.2 | async-start | bytes 262144 | tf_op jit(solution)/shard_map/all_to_all | solution.py:501
